TPU v7x, 256 devices: a whole 4x4x8 slice. The times are simulated.
256 devices in a mesh: ia: 8 (over z), ja: 8 (over x, core), ka: 4 (over y).
Axes of the slice: x: 4, y: 4, z: 8, core: 2. Of those that a mesh axis runs over, the one named last changes fastest.
Arguments:
- tensor: float32 [1024, 1024, 512], P('ia', 'ja', 'ka'), may hold values from -6000 to 6000
- factor_b: float32 [1024, 256], P(('ja', 'ia', 'ka')), may hold values from -6 to 6
- factor_c: float32 [512, 256], P(('ka', 'ia', 'ja')), may hold values from -6 to 6
Outputs:
- new_a: float32 [1024, 256], P(('ia', 'ja', 'ka'))
- new_b: float32 [1024, 256], P(('ja', 'ia', 'ka'))
- new_c: float32 [512, 256], P(('ka', 'ia', 'ja'))
All inputs are finite; a program needn't handle non-finite values.
Results may differ from a plain program's by a relative error of at most 0.0003.
Values sent between devices are 32-bit elements; how exact they have to be, the bound alone decides.
A program may use at most 128 MiB of HBM per device.

v0:
```python
import jax
import jax.numpy as jnp
from jax import lax
from jax.sharding import PartitionSpec as P


def contract(form, left, right):
    return jnp.einsum(form, left, right, precision=lax.Precision.HIGHEST)


def gram_of(rows):
    return contract("nr,ns->rs", rows, rows)


def solve_rows(rows, hadamard):
    factor = jnp.linalg.cholesky(hadamard)
    return jax.scipy.linalg.cho_solve((factor, True), rows.T).T


def column_scale(gram_matrix, count):
    return jnp.sqrt(jnp.diagonal(gram_matrix) / count + 1e-06)


def gather_first(rows):
    return lax.all_gather(rows, ("ja", "ka"), axis=0, tiled=True)


def gather_second(rows):
    return lax.all_gather(rows, ("ia", "ka"), axis=0, tiled=True)


def per_device(tensor, factor_b, factor_c):
    count_i = tensor.shape[0] * lax.axis_size("ia")
    count_j = tensor.shape[1] * lax.axis_size("ja")
    count_k = tensor.shape[2] * lax.axis_size("ka")
    block_b = lax.all_gather(factor_b, ("ia", "ka"), axis=0, tiled=True)
    block_c = lax.all_gather(factor_c, ("ia", "ja"), axis=0, tiled=True)
    gram_b, gram_c = lax.psum((gram_of(factor_b), gram_of(factor_c)), ("ia", "ja", "ka"))
    piece = tensor
    rows_a = lax.psum_scatter(
        contract("ikr,kr->ir", contract("ijk,jr->ikr", piece, block_b), block_c),
        ("ja", "ka"),
        scatter_dimension=0,
        tiled=True,
    )
    raw_a = solve_rows(rows_a, gram_b * gram_c)
    gram_ra = lax.psum(gram_of(raw_a), ("ia", "ja", "ka"))
    scale_a = column_scale(gram_ra, count_i)
    new_a = raw_a / scale_a
    block_a = gather_first(new_a)
    gram_a = gram_ra / (scale_a[:, None] * scale_a[None, :])
    second_first = jnp.transpose(tensor, (1, 0, 2))
    piece = second_first
    rows_b = lax.psum_scatter(
        contract("jir,ir->jr", contract("jik,kr->jir", piece, block_c), block_a),
        ("ia", "ka"),
        scatter_dimension=0,
        tiled=True,
    )
    raw_b = solve_rows(rows_b, gram_a * gram_c)
    gram_rb = lax.psum(gram_of(raw_b), ("ia", "ja", "ka"))
    scale_b = column_scale(gram_rb, count_j)
    new_b = raw_b / scale_b
    block_nb = gather_second(new_b)
    gram_nb = gram_rb / (scale_b[:, None] * scale_b[None, :])
    third_first = jnp.transpose(tensor, (2, 0, 1))
    piece = third_first
    rows_c = lax.psum_scatter(
        contract("kjr,jr->kr", contract("kij,ir->kjr", piece, block_a), block_nb),
        ("ia", "ja"),
        scatter_dimension=0,
        tiled=True,
    )
    raw_c = solve_rows(rows_c, gram_a * gram_nb)
    norms = lax.psum(jnp.sum(raw_c * raw_c, axis=0), ("ia", "ja", "ka"))
    new_c = raw_c / jnp.sqrt(norms / count_k + 1e-06)
    return (new_a, new_b, new_c)


def solution(mesh):
    return jax.shard_map(
        per_device,
        mesh=mesh,
        in_specs=(P("ia", "ja", "ka"), P(("ja", "ia", "ka"), None), P(("ka", "ia", "ja"), None)),
        out_specs=(
            P(("ia", "ja", "ka"), None),
            P(("ja", "ia", "ka"), None),
            P(("ka", "ia", "ja"), None),
        ),
        check_vma=False,
    )
```

profile of v0, /device:TPU:1, one launch (start us, length us, event | category | flops | bytes accessed | tf_op | source)
XLA Modules:
  0.0 1606.4 jit_solution(5378691764918174224)
XLA Ops:
  7.2 54.1 %all-gather.1 = f32[64,2,256]{2,1,0:T(2,128)S(1)} all-gather(f32[1,2,256]{2,1,0:T(2,128)} %bitcast.175), channel_id=1, replica_groups=mesh['ia'=8,'ja'=8,'ka'=4] {'ia','ja'}, dimensions={0}, use_global_device_ids=true | all-gather | bytes 133120 | tf_op jit(solution)/shard_map/all_gather | solution.py:37
  61.4 33.0 %all-gather = f32[32,4,256]{2,1,0:T(4,128)S(1)} all-gather(f32[1,4,256]{2,1,0:T(4,128)} %bitcast.174), channel_id=1, replica_groups=mesh['ia'=8,'ja'=8,'ka'=4] {'ia','ka'}, dimensions={0}, use_global_device_ids=true | all-gather | bytes 135168 | tf_op jit(solution)/shard_map/all_gather | solution.py:36
  94.5 15.6 multiply_reduce_fusion.1
  110.1 0.8 copy.57
  111.0 1.1 fusion.50
  112.1 1.1 fusion.51
  114.8 112.2 %all-reduce.16.cloned.1.call-done = f32[128,256]{0,1:T(8,128)} async-done(((f32[128,256]{0,1:T(8,128)}), f32[128,256]{0,1:T(8,128)}) %all-reduce.16.cloned.1.call-update) | async-done | bytes 131088
  227.0 1.0 constant_dynamic-slice_fusion.5
  228.0 256.4 %all-reduce.22.cloned.1.call-done = (f32[256,256]{0,1:T(8,128)}, f32[256,256]{0,1:T(8,128)}) async-done(((f32[256,256]{0,1:T(8,128)}, f32[256,256]{0,1:T(8,128)}), (f32[256,256]{0,1:T(8,128)}, f32[256,256]{0,1:T(8,128)})) %all-reduce.22.cloned.1.call-update) | async-done | bytes 524304 | tf_op jit(solution)/shard_map/psum | solution.py:38
  484.4 1.1 mul.39
  485.7 11.7 cholesky.172
  497.4 9.8 custom-call.28
  507.8 11.7 cholesky.189
  519.5 0.7 compare_reduce_fusion.4
  521.6 4.4 while.6
  522.6 1.4 bitcast_dynamic-update-slice_fusion.7
  524.6 1.4 bitcast_dynamic-update-slice_fusion.7
  526.0 19.7 %custom-call.29 = f32[2,128,128]{1,2,0:T(8,128)S(1)} custom-call(f32[2,128,128]{2,1,0:T(8,128)S(1)} %get-tuple-element.27), custom_call_target="InvertDiagBlocksLowerTriangular" | custom-call | tf_op jit(solution)/shard_map/jit(_cho_solve)/triangular_solve | solution.py:17
  546.8 1.2 fusion.37
  548.2 0.6 dynamic-slice.10
  549.4 247.7 %all-reduce.12.cloned.1.call-done = f32[256,256]{0,1:T(8,128)} async-done(((f32[256,256]{0,1:T(8,128)}), f32[256,256]{0,1:T(8,128)}) %all-reduce.12.cloned.1.call-update) | async-done | bytes 262160 | tf_op jit(solution)/shard_map/psum | solution.py:47
  797.2 2.6 gather_fusion
  799.8 0.6 fusion.43
  800.4 38.2 %all-gather.2 = f32[32,4,256]{2,1,0:T(4,128)S(1)} all-gather(f32[1,4,256]{2,1,0:T(4,128)S(1)} %get-tuple-element.75), channel_id=1, replica_groups=mesh['ia'=8,'ja'=8,'ka'=4] {'ja','ka'}, dimensions={0}, use_global_device_ids=true | all-gather | bytes 135168 | tf_op jit(solution)/shard_map/all_gather | solution.py:25
  838.6 15.7 multiply_reduce_fusion
  854.3 0.7 copy.65
  855.7 11.7 cholesky.206
  867.4 0.7 compare_reduce_fusion.3
  868.1 9.8 custom-call.30
  878.4 11.7 cholesky.223
  890.2 0.6 compare_reduce_fusion.2
  892.1 4.1 while.7
  892.2 0.7 fusion.86
  892.8 1.3 bitcast_dynamic-update-slice_fusion.8
  894.2 0.7 fusion.86
  894.9 1.3 bitcast_dynamic-update-slice_fusion.8
  896.2 19.7 %custom-call.31 = f32[2,128,128]{1,2,0:T(8,128)S(1)} custom-call(f32[2,128,128]{2,1,0:T(8,128)S(1)} %get-tuple-element.28), custom_call_target="InvertDiagBlocksLowerTriangular" | custom-call | tf_op jit(solution)/shard_map/jit(_cho_solve)/triangular_solve | solution.py:17
  915.9 75.6 %all-reduce.18.cloned.1.call-done = f32[128,256]{0,1:T(8,128)} async-done(((f32[128,256]{0,1:T(8,128)}), f32[128,256]{0,1:T(8,128)}) %all-reduce.18.cloned.1.call-update) | async-done | bytes 131088
  991.5 1.0 constant_dynamic-slice_fusion.4
  993.7 1.2 fusion.35
  995.0 0.6 dynamic-slice.12
  995.6 9.3 copy.46
  1005.5 242.0 %all-reduce.14.cloned.1.call-done = f32[256,256]{0,1:T(8,128)} async-done(((f32[256,256]{0,1:T(8,128)}), f32[256,256]{0,1:T(8,128)}) %all-reduce.14.cloned.1.call-update) | async-done | bytes 262160 | tf_op jit(solution)/shard_map/psum | solution.py:61
  1247.6 2.6 gather_fusion.1
  1250.2 0.6 fusion.45
  1250.8 34.2 %all-gather.3 = f32[32,4,256]{2,1,0:T(4,128)S(1)} all-gather(f32[1,4,256]{2,1,0:T(4,128)S(1)} %get-tuple-element.73), channel_id=1, replica_groups=mesh['ia'=8,'ja'=8,'ka'=4] {'ia','ka'}, dimensions={0}, use_global_device_ids=true | all-gather | bytes 135168 | tf_op jit(solution)/shard_map/all_gather | solution.py:29
  1285.1 1.1 divide_multiply_fusion
  1286.4 11.7 cholesky.240
  1298.1 0.6 compare_reduce_fusion.1
  1298.8 9.8 custom-call.32
  1309.1 11.7 cholesky.257
  1320.8 0.7 compare_reduce_fusion
  1321.5 18.5 %fusion = f32[256,128]{0,1:T(8,128)S(1)} fusion(f32[128,128,128]{2,1,0:T(8,128)} %copy.46, f32[256,128]{1,0:T(8,128)S(1)} %copy.84, f32[128,256]{1,0:T(8,128)S(1)} %reshape.116), kind=kOutput, calls=%fused_computation.9 | convolution fusion | flops 6450806784 | bytes 8781824 | tf_op jit(solution)/shard_map/kij,ir->kjr/dot_general | solution.py:8
  1340.0 0.8 copy.74
  1342.1 4.0 while.5
  1342.1 0.6 fusion.84
  1342.7 1.3 bitcast_dynamic-update-slice_fusion.6
  1344.1 0.6 fusion.84
  1344.8 1.3 bitcast_dynamic-update-slice_fusion.6
  1346.1 19.7 %custom-call.20 = f32[2,128,128]{1,2,0:T(8,128)S(1)} custom-call(f32[2,128,128]{2,1,0:T(8,128)S(1)} %get-tuple-element.20), custom_call_target="InvertDiagBlocksLowerTriangular" | custom-call | tf_op jit(solution)/shard_map/jit(_cho_solve)/triangular_solve | solution.py:17
  1365.8 155.9 %all-reduce.20.cloned.1.call-done = f32[128,256]{0,1:T(8,128)} async-done(((f32[128,256]{0,1:T(8,128)}), f32[128,256]{0,1:T(8,128)}) %all-reduce.20.cloned.1.call-update) | async-done | bytes 131088
  1521.7 1.0 constant_dynamic-slice_fusion.3
  1524.0 74.6 %psum.39 = f32[256]{0:T(256)S(1)} all-reduce(f32[256]{0:T(256)S(1)} %multiply_reduce_fusion.2), channel_id=1, replica_groups=mesh['ia'=8,'ja'=8,'ka'=4] {'ia','ja','ka'}, use_global_device_ids=true, to_apply=%region_12.15 | all-reduce | flops 256 | bytes 2048 | tf_op jit(solution)/shard_map/psum | solution.py:75
  1598.6 0.6 divide_bitcast_fusion
  (100 shorter events, 9.2 us)
Async XLA Ops:
  7.2 106.4 %copy-start.6 = (u32[256]{0:T(256)S(1)}, u32[256]{0:T(256)}, u32[]{:S(2)}) copy-start(u32[256]{0:T(256)} %constant.170) | copy-start | bytes 3076
  7.2 104.9 %copy-start.3 = (f32[2,256]{1,0:T(2,128)S(1)}, f32[2,256]{1,0:T(2,128)}, u32[]{:S(2)}) copy-start(f32[2,256]{1,0:T(2,128)} %param.8) | copy-start | bytes 6148
  7.2 103.8 %copy-start.2 = (f32[4,256]{1,0:T(4,128)S(1)}, f32[4,256]{1,0:T(4,128)}, u32[]{:S(2)}) copy-start(f32[4,256]{1,0:T(4,128)} %param.7) | copy-start | bytes 12292
  7.2 219.8 %all-reduce.16.cloned.1.call-start = ((), (), s32[]{:S(2)}) async-start(), calls=%async_computation.2 | async-start | bytes 262144
  94.5 453.7 %copy-start.5 = (u32[256]{0:T(256)S(1)}, u32[256]{0:T(256)}, u32[]{:S(2)}) copy-start(u32[256]{0:T(256)} %constant.174) | copy-start | bytes 3076
  110.9 373.5 %all-reduce.22.cloned.1.call-start = ((), (), s32[]{:S(2)}) async-start(), calls=%async_computation.5 | async-start | bytes 1048576 | tf_op jit(solution)/shard_map/psum | solution.py:38
  113.3 683.9 %all-reduce.12.cloned.1.call-start = ((), (), s32[]{:S(2)}) async-start(), calls=%async_computation | async-start | bytes 524288 | tf_op jit(solution)/shard_map/psum | solution.py:47
  548.0 443.5 %all-reduce.18.cloned.1.call-start = ((), (), s32[]{:S(2)}) async-start(), calls=%async_computation.3 | async-start | bytes 262144
  799.8 55.6 %copy-start = (f32[256,256]{0,1:T(8,128)S(1)}, f32[256,256]{0,1:T(8,128)}, u32[]{:S(2)}) copy-start(f32[256,256]{0,1:T(8,128)} %all-reduce.12.cloned.1.call-done) | copy-start | bytes 786436
  799.8 55.6 %copy-start.1 = (f32[256,256]{0,1:T(8,128)S(1)}, f32[256,256]{0,1:T(8,128)}, u32[]{:S(2)}) copy-start(f32[256,256]{0,1:T(8,128)} %get-tuple-element.54) | copy-start | bytes 786436
  838.6 156.4 %copy-start.4 = (u32[256]{0:T(256)S(1)}, u32[256]{0:T(256)}, u32[]{:S(2)}) copy-start(u32[256]{0:T(256)} %constant.178) | copy-start | bytes 3076
  855.1 392.5 %all-reduce.14.cloned.1.call-start = ((), (), s32[]{:S(2)}) async-start(), calls=%async_computation.1 | async-start | bytes 524288 | tf_op jit(solution)/shard_map/psum | solution.py:61
  994.9 526.7 %all-reduce.20.cloned.1.call-start = ((), (), s32[]{:S(2)}) async-start(), calls=%async_computation.4 | async-start | bytes 262144
Sparse Core Ops, SparseCore 0:
  111.0 115.8 all-reduce.15
  233.5 250.8 all-reduce.21
  548.1 248.9 all-reduce.11
  855.2 136.2 all-reduce.17
  996.8 250.7 all-reduce.13
  1340.9 180.6 all-reduce.19
where the time goes:
time: 1610 us
  waiting for transfers between devices  1090 us (68%)
  blocking collectives  234 us (15%)
  other arithmetic  167 us (10%)
  matrix products  59.4 us (4%)
  local copies, waits for them, and re-layouts  34.6 us (2%)
  between operations  20.7 us (1%)
    unnamed x9, waiting for transfers between devices  344 us
    psum x1, waiting for transfers between devices, per_device(): lax.psum((gram_of(factor_b), gram_of(factor_c)), ('ia', 'ja', 'ka'))  256 us
    psum x1, waiting for transfers between devices, per_device(): gram_ra = lax.psum(gram_of(raw_a), ('ia', 'ja', 'ka'))  248 us
    psum x1, waiting for transfers between devices, per_device(): gram_rb = lax.psum(gram_of(raw_b), ('ia', 'ja', 'ka'))  242 us
    another operation x20, other arithmetic, solve_rows(): factor = jnp.linalg.cholesky(hadamard)  103 us
    psum x1, blocking collectives, per_device(): norms = lax.psum(jnp.sum(raw_c * raw_c, axis=0), ('ia', 'ja', 'ka'))  74.6 us
    another operation x7, other arithmetic, solve_rows(): return jax.scipy.linalg.cho_solve((factor, True), rows.T).T  59.1 us
    dot_general x7, matrix products, contract(): return jnp.einsum(form, left, right, precision=lax.Precision.HIGHEST)  54.6 us
  transfers between devices with their start and end apart: 6, of which 6 were waited for; matrix products, arithmetic and copies ran while one was open for 6% of the time, Pallas kernels for 0%

commit v1 on v0

v1 whole, which is shorter than its diff:
```python
import functools

import jax
import jax.numpy as jnp
from jax import lax
from jax.experimental import pallas as pl
from jax.experimental.pallas import tpu as pltpu
from jax.sharding import PartitionSpec as P

MESH = pl.DeviceIdType.MESH
F32 = jnp.float32
BF16 = jnp.bfloat16
HIGHEST = lax.Precision.HIGHEST
PIV = 32
GROUP = 8


def split(v):
    hi = v.astype(BF16)
    lo = (v - hi.astype(F32)).astype(BF16)
    return hi, lo


def stack_split(v):
    hi, lo = split(v)
    return jnp.concatenate([hi, hi], axis=0), jnp.concatenate([lo, lo], axis=0)


def mxu(left, right):
    return jnp.dot(left, right, preferred_element_type=F32)


def dot_full(left, right):
    return jnp.dot(left, right, preferred_element_type=F32, precision=HIGHEST)


def gram_of(rows):
    return lax.dot_general(
        rows, rows, (((0,), (0,)), ((), ())), preferred_element_type=F32, precision=HIGHEST
    )


def diagonals(matrix):
    n = matrix.shape[0]
    row = lax.broadcasted_iota(jnp.int32, (n, n), 0)
    col = lax.broadcasted_iota(jnp.int32, (n, n), 1)
    only = jnp.where(row == col, matrix, 0.0)
    return jnp.sum(only, axis=0, keepdims=True), jnp.sum(only, axis=1, keepdims=True)


def sweep_step(mat):
    n = mat.shape[0]
    front = mat[0:PIV, :]
    panel = front
    sub = lax.broadcasted_iota(jnp.int32, (PIV, n), 0)
    lane = lax.broadcasted_iota(jnp.int32, (PIV, n), 1)
    for p in range(PIV):
        col = panel[:, p : p + 1]
        inverse = 1.0 / panel[p : p + 1, p : p + 1]
        unit = jnp.where(lane == p, jnp.where(sub == p, 1.0, 0.0), panel)
        row = unit[p : p + 1, :] * inverse
        panel = jnp.where(sub == p, row, unit - col * row)
    wide = jnp.concatenate([panel, jnp.zeros((128 - PIV, n), F32)], axis=0)
    tall = wide.T
    front_wide = jnp.concatenate([front, jnp.zeros((128 - PIV, n), F32)], axis=0)
    rest = mat[PIV:, :] - dot_full(tall[PIV:, :], front_wide)
    tall_wide = jnp.concatenate([tall[PIV:, :], jnp.zeros((n - PIV, n - 128), F32)], axis=1)
    rest_lane = lax.broadcasted_iota(jnp.int32, (n - PIV, n), 1)
    rest = jnp.where(rest_lane < PIV, tall_wide, rest)
    top = jnp.where(lane < PIV, -panel, panel)
    mat_new = jnp.concatenate([rest, top], axis=0)
    return pltpu.roll(mat_new, n - PIV, 1)


def invert_in(ref):
    n = ref.shape[0]

    def step(_, carry):
        ref[...] = sweep_step(ref[...])
        return carry

    lax.fori_loop(0, n // PIV, step, 0)


def kernel(
    ni, nj, nk, counts,
    x_hbm, b_ref, c_ref, oa_ref, ob_ref, oc_ref,
    xs, xt, ys, bin_, cin, bblk, cblk, ablk, nblk, whi, wlo, rows, arow,
    part_ab, part_b, part_c, recv_a, recv_b, recv_c, own_a, own_b, gat_a, gat_b,
    gp_b, gp_c, gp_a, gp_n, ex_b, ex_c, ex_a, ex_n, sum_b, sum_c, sum_a, sum_n,
    g_b, g_c, g_a, g_n, hmat, gca, nrm1, nrm2, own_n1, own_n2,
    ss, rs, xsem,
):
    rank = b_ref.shape[1]
    nblkrows = 128
    ia, ja, ka = lax.axis_index("ia"), lax.axis_index("ja"), lax.axis_index("ka")
    n_a, n_b, n_c, n_d = nj * nk, ni * nk, ni * nj, ni * nj // 2
    me_a, me_b, me_c, me_d = ja * nk + ka, ia * nk + ka, ia * nj + ja, ia * (nj // 2) + ja // 2

    def peer_a(q):
        return {"ia": ia, "ja": q // nk, "ka": lax.rem(q, nk)}

    def peer_b(q):
        return {"ia": q // nk, "ja": ja, "ka": lax.rem(q, nk)}

    def peer_c(q):
        return {"ia": q // nj, "ja": lax.rem(q, nj), "ka": ka}

    def peer_d(q):
        return {"ia": q // (nj // 2), "ja": lax.rem(q, nj // 2) * 2 + lax.rem(ja, 2), "ka": ka}

    def line_i(q):
        return {"ia": q, "ja": ja, "ka": ka}

    def line_j(q):
        return {"ia": ia, "ja": q, "ka": ka}

    def line_k(q):
        return {"ia": ia, "ja": ja, "ka": q}

    def send(phase, n, me, peer, src_of, dst):
        def go(p, carry):
            q = lax.rem(me + p, n)
            pltpu.make_async_remote_copy(
                src_ref=src_of(q), dst_ref=dst, send_sem=ss.at[phase], recv_sem=rs.at[phase],
                device_id=peer(q), device_id_type=MESH,
            ).start()
            return carry
        lax.fori_loop(1, n, go, 0)

    def all_of(phase, n, me, peer, buf):
        some = buf.at[pl.ds(0, n - 1)]
        return pltpu.make_async_remote_copy(
            src_ref=some, dst_ref=some, send_sem=ss.at[phase], recv_sem=rs.at[phase],
            device_id=peer(lax.rem(me + 1, n)), device_id_type=MESH,
        )

    def assemble(dst, src):
        n, per = src.shape[0], src.shape[1]
        for s in range(n):
            dst[s * per : (s + 1) * per, :] = src[s]

    def scatter_out(dst, src):
        n, per = dst.shape[0], dst.shape[1]
        for s in range(n):
            dst[s] = src[s * per : (s + 1) * per, :]

    xcopy = pltpu.make_async_copy(x_hbm, xs, xsem)
    xcopy.start()
    barrier = pltpu.get_barrier_semaphore()

    def hello(n, me, peer):
        def go(p, carry):
            pl.semaphore_signal(barrier, inc=1, device_id=peer(lax.rem(me + p, n)), device_id_type=MESH)
            return carry
        lax.fori_loop(1, n, go, 0)

    hello(n_a, me_a, peer_a)

    def other_i(p, carry):
        i2 = lax.rem(ia + p, ni)

        def along_j(j2, c2):
            pl.semaphore_signal(barrier, inc=1, device_id={"ia": i2, "ja": j2, "ka": ka}, device_id_type=MESH)
            return c2
        lax.fori_loop(0, nj, along_j, 0)

        def along_k(k2, c2):
            pl.semaphore_signal(
                barrier, inc=1, device_id={"ia": i2, "ja": ja, "ka": lax.rem(ka + k2, nk)}, device_id_type=MESH
            )
            return c2
        lax.fori_loop(1, nk, along_k, 0)
        return carry
    lax.fori_loop(1, ni, other_i, 0)
    pl.semaphore_wait(barrier, (n_a - 1) + (ni - 1) * (nj + nk - 1))

    bin_[me_b] = b_ref[...]
    cin[me_c] = c_ref[...]
    send(0, n_b, me_b, peer_b, lambda q: b_ref, bin_.at[me_b])
    send(1, n_c, me_c, peer_c, lambda q: c_ref, cin.at[me_c])

    xcopy.wait()

    def turn(j, carry):
        hi, lo = split(xs[pl.ds(j, nblkrows, stride=nblkrows), :].T)
        at = pl.ds(pl.multiple_of(j * nblkrows, nblkrows), nblkrows)
        xt[at, 0:128] = hi
        xt[at, 128:256] = lo
        return carry
    lax.fori_loop(0, 128, turn, 0, unroll=4)

    all_of(0, n_b, me_b, peer_b, bin_).wait_recv()
    all_of(1, n_c, me_c, peer_c, cin).wait_recv()
    assemble(bblk, bin_)
    assemble(cblk, cin)

    def gram_slices(dst, blk):
        dst[...] = gram_of(blk[...]).reshape(dst.shape)

    gram_slices(gp_b, bblk)
    gram_slices(gp_c, cblk)
    ex_b[ja] = gp_b[me_b]
    send(2, nj, ja, line_j, lambda q: gp_b.at[me_b], ex_b.at[ja])
    ex_c[ka] = gp_c[me_d]
    send(3, nk, ka, line_k, lambda q: gp_c.at[me_d], ex_c.at[ka])

    whi[...], wlo[...] = stack_split(cblk[...])
    step_rows = GROUP * nblkrows

    def mode_one(g, carry):
        at = pl.ds(pl.multiple_of(g * step_rows, step_rows), step_rows)
        hi, lo = split(xs[at, :])
        both = jnp.concatenate([hi, lo], axis=1)
        y = mxu(both, whi[...]) + mxu(both, wlo[...])
        ys[at, :] = y
        terms = y.reshape(GROUP, nblkrows, rank) * bblk[...][None]
        rows[pl.ds(pl.multiple_of(g * GROUP, GROUP), GROUP), :] = jnp.sum(terms, axis=1)
        return carry

    steps = 128 // GROUP
    lax.fori_loop(0, steps // 2, mode_one, 0)

    def finish_gram(phase, n, me, line, ex, own, n_p, me_p, peer, full):
        all_of(phase, n, me, line, ex).wait_recv()
        total = jnp.sum(ex[...], axis=0)
        own[...] = total
        full[me_p] = total
        send(phase + 2, n_p, me_p, peer, lambda q: own, full.at[me_p])

    finish_gram(2, nj, ja, line_j, ex_b, sum_b, n_b, me_b, peer_b, g_b)
    finish_gram(3, nk, ka, line_k, ex_c, sum_c, n_d, me_d, peer_d, g_c)
    lax.fori_loop(steps // 2, steps, mode_one, 0)

    scatter_out(part_ab, rows)
    recv_a[me_a] = part_ab[me_a]
    send(6, n_a, me_a, peer_a, lambda q: part_ab.at[q], recv_a.at[me_a])

    all_of(4, n_b, me_b, peer_b, g_b).wait_recv()
    all_of(5, n_d, me_d, peer_d, g_c).wait_recv()
    hmat[...] = g_b[...].reshape(rank, rank) * g_c[...].reshape(rank, rank)
    invert_in(hmat)

    def solve(summed):
        per = summed.shape[0]
        if per < 8:
            summed = jnp.concatenate([summed, jnp.zeros((8 - per, rank), F32)], axis=0)
        return -dot_full(summed, hmat[...])[0:per]

    all_of(6, n_a, me_a, peer_a, recv_a).wait_recv()
    own_a[...] = solve(jnp.sum(recv_a[...], axis=0))
    gat_a[me_a] = own_a[...]
    send(7, n_a, me_a, peer_a, lambda q: own_a, gat_a.at[me_a])
    all_of(7, n_a, me_a, peer_a, gat_a).wait_recv()
    assemble(ablk, gat_a)

    gram_slices(gp_a, ablk)
    ex_a[ia] = gp_a[me_a]
    send(8, ni, ia, line_i, lambda q: gp_a.at[me_a], ex_a.at[ia])

    def sum_rows(factor):
        def add(s, total):
            at = pl.ds(pl.multiple_of(s * nblkrows, nblkrows), nblkrows)
            return total + ys[at, :] * factor[pl.ds(s, 1), :]
        return lax.fori_loop(0, 128, add, jnp.zeros((nblkrows, rank), F32), unroll=8)

    rows[...] = sum_rows(ablk)
    scatter_out(part_b, rows)
    recv_b[me_b] = part_b[me_b]
    send(10, n_b, me_b, peer_b, lambda q: part_b.at[q], recv_b.at[me_b])

    all_of(8, ni, ia, line_i, ex_a).wait_recv()
    total_a = jnp.sum(ex_a[...], axis=0)
    sum_a[...] = total_a
    g_a[me_a] = total_a
    send(9, n_a, me_a, peer_a, lambda q: sum_a, g_a.at[me_a])

    whi[...], wlo[...] = stack_split(ablk[...])

    def third(g, carry):
        at = pl.ds(pl.multiple_of(g * step_rows, step_rows), step_rows)
        both = xt[at, :]
        ys[at, :] = mxu(both, whi[...]) + mxu(both, wlo[...])
        return carry
    lax.fori_loop(0, steps, third, 0)

    all_of(9, n_a, me_a, peer_a, g_a).wait_recv()
    gram = g_a[...].reshape(rank, rank)
    along, down = diagonals(gram)
    scale_a = jnp.sqrt(along / counts[0] + 1e-06)
    inverse_a = 1.0 / scale_a
    gca[...] = (gram * inverse_a) * (1.0 / jnp.sqrt(down / counts[0] + 1e-06))
    hmat[...] = gca[...] * g_c[...].reshape(rank, rank)
    oa_ref[...] = own_a[...] / scale_a
    arow[...] = inverse_a
    invert_in(hmat)

    all_of(10, n_b, me_b, peer_b, recv_b).wait_recv()
    own_b[...] = solve(jnp.sum(recv_b[...], axis=0) * arow[...])
    gat_b[me_b] = own_b[...]
    send(11, n_b, me_b, peer_b, lambda q: own_b, gat_b.at[me_b])
    all_of(11, n_b, me_b, peer_b, gat_b).wait_recv()
    assemble(nblk, gat_b)

    gram_slices(gp_n, nblk)
    ex_n[ja] = gp_n[me_b]
    send(12, nj, ja, line_j, lambda q: gp_n.at[me_b], ex_n.at[ja])

    nblk[...] = nblk[...] * arow[...]
    rows[...] = sum_rows(nblk)
    scatter_out(part_c, rows)
    recv_c[me_c] = part_c[me_c]
    send(14, n_c, me_c, peer_c, lambda q: part_c.at[q], recv_c.at[me_c])

    all_of(12, nj, ja, line_j, ex_n).wait_recv()
    total_n = jnp.sum(ex_n[...], axis=0)
    sum_n[...] = total_n
    g_n[me_b] = total_n
    send(13, n_b, me_b, peer_b, lambda q: sum_n, g_n.at[me_b])
    all_of(13, n_b, me_b, peer_b, g_n).wait_recv()
    gram = g_n[...].reshape(rank, rank)
    along, down = diagonals(gram)
    scale_b = jnp.sqrt(along / counts[1] + 1e-06)
    inverse_b = 1.0 / scale_b
    hmat[...] = gca[...] * ((gram * inverse_b) * (1.0 / jnp.sqrt(down / counts[1] + 1e-06)))
    ob_ref[...] = own_b[...] / scale_b
    arow[...] = inverse_b
    invert_in(hmat)

    all_of(14, n_c, me_c, peer_c, recv_c).wait_recv()
    raw_c = solve(jnp.sum(recv_c[...], axis=0) * arow[...])
    squares = jnp.sum(raw_c * raw_c, axis=0, keepdims=True)
    own_n1[...] = squares
    nrm1[ia] = squares
    send(15, ni, ia, line_i, lambda q: own_n1, nrm1.at[ia])
    all_of(15, ni, ia, line_i, nrm1).wait_recv()
    squares = jnp.sum(nrm1[...], axis=0)
    own_n2[...] = squares
    nrm2[me_a] = squares
    send(16, n_a, me_a, peer_a, lambda q: own_n2, nrm2.at[me_a])
    all_of(16, n_a, me_a, peer_a, nrm2).wait_recv()
    squares = jnp.sum(nrm2[...], axis=0)
    oc_ref[...] = raw_c / jnp.sqrt(squares / counts[2] + 1e-06)

    for phase, n, me, peer, buf in (
        (0, n_b, me_b, peer_b, bin_), (1, n_c, me_c, peer_c, cin),
        (2, nj, ja, line_j, ex_b), (3, nk, ka, line_k, ex_c),
        (4, n_b, me_b, peer_b, g_b), (5, n_d, me_d, peer_d, g_c),
        (6, n_a, me_a, peer_a, recv_a), (7, n_a, me_a, peer_a, gat_a),
        (8, ni, ia, line_i, ex_a), (9, n_a, me_a, peer_a, g_a),
        (10, n_b, me_b, peer_b, recv_b), (11, n_b, me_b, peer_b, gat_b),
        (12, nj, ja, line_j, ex_n), (13, n_b, me_b, peer_b, g_n),
        (14, n_c, me_c, peer_c, recv_c), (15, ni, ia, line_i, nrm1),
        (16, n_a, me_a, peer_a, nrm2),
    ):
        all_of(phase, n, me, peer, buf).wait_send()


def per_device(ni, nj, nk, tensor, factor_b, factor_c):
    counts = (tensor.shape[0] * ni, tensor.shape[1] * nj, tensor.shape[2] * nk)
    rank = factor_b.shape[1]
    n_a, n_b, n_c, n_d = nj * nk, ni * nk, ni * nj, ni * nj // 2
    r_a, r_b, r_c = 128 // n_a, 128 // n_b, 128 // n_c
    v = lambda *shape: pltpu.VMEM(shape, F32)
    scratch = [
        v(16384, 128), pltpu.VMEM((16384, 256), BF16), v(16384, rank),
        v(n_b, r_b, rank), v(n_c, r_c, rank),
        v(128, rank), v(128, rank), v(128, rank), v(128, rank),
        pltpu.VMEM((256, rank), BF16), pltpu.VMEM((256, rank), BF16),
        v(128, rank), v(1, rank),
        v(n_a, r_a, rank), v(n_b, r_b, rank), v(n_c, r_c, rank),
        v(n_a, r_a, rank), v(n_b, r_b, rank), v(n_c, r_c, rank),
        v(r_a, rank), v(r_b, rank), v(n_a, r_a, rank), v(n_b, r_b, rank),
        v(n_b, rank // n_b, rank), v(n_d, rank // n_d, rank),
        v(n_a, rank // n_a, rank), v(n_b, rank // n_b, rank),
        v(nj, rank // n_b, rank), v(nk, rank // n_d, rank),
        v(ni, rank // n_a, rank), v(nj, rank // n_b, rank),
        v(rank // n_b, rank), v(rank // n_d, rank), v(rank // n_a, rank), v(rank // n_b, rank),
        v(n_b, rank // n_b, rank), v(n_d, rank // n_d, rank),
        v(n_a, rank // n_a, rank), v(n_b, rank // n_b, rank),
        v(rank, rank), v(rank, rank),
        v(ni, 1, rank), v(n_a, 1, rank), v(1, rank), v(1, rank),
        pltpu.SemaphoreType.DMA((17,)), pltpu.SemaphoreType.DMA((17,)), pltpu.SemaphoreType.DMA,
    ]
    vmem = pl.BlockSpec(memory_space=pltpu.VMEM)
    return pl.pallas_call(
        functools.partial(kernel, ni, nj, nk, counts),
        out_shape=(
            jax.ShapeDtypeStruct((r_a, rank), F32),
            jax.ShapeDtypeStruct((r_b, rank), F32),
            jax.ShapeDtypeStruct((r_c, rank), F32),
        ),
        in_specs=[pl.BlockSpec(memory_space=pl.ANY), vmem, vmem],
        out_specs=(vmem, vmem, vmem),
        scratch_shapes=scratch,
        compiler_params=pltpu.CompilerParams(
            collective_id=0, has_side_effects=True, vmem_limit_bytes=52 * 1024 * 1024
        ),
    )(tensor.reshape(16384, 128), factor_b, factor_c)


def solution(mesh):
    ni, nj, nk = mesh.shape["ia"], mesh.shape["ja"], mesh.shape["ka"]
    return jax.shard_map(
        functools.partial(per_device, ni, nj, nk),
        mesh=mesh,
        in_specs=(P("ia", "ja", "ka"), P(("ja", "ia", "ka"), None), P(("ka", "ia", "ja"), None)),
        out_specs=(
            P(("ia", "ja", "ka"), None),
            P(("ja", "ia", "ka"), None),
            P(("ka", "ia", "ja"), None),
        ),
        check_vma=False,
    )
```

time: 1610 us -> 172 us (0.11)
  waiting for transfers between devices: 1090 us -> 0 us
  blocking collectives: 234 us -> 0 us
  Pallas kernels: 0 us -> 168 us
  other arithmetic: 167 us -> 0 us
  matrix products: 59.4 us -> 0 us
  local copies, waits for them, and re-layouts: 34.6 us -> 3.13 us
  between operations: 20.7 us -> 0.65 us
    psum x3 -> x0, waiting for transfers between devices: 746 us -> none  [the longest x1 256 us: per_device(): lax.psum((gram_of(factor_b), gram_of(factor_c)), ('ia', 'ja', 'ka'))]
    unnamed x9 -> x0, waiting for transfers between devices: 344 us -> none
    pallas_call x0 -> x1, Pallas kernels: none -> 168 us  [per_device(): pl.pallas_call(functools.partial(kernel, ni, nj, nk, counts), out_shape=(...]
    another operation x27 -> x0, other arithmetic: 162 us -> none  [the longest x20 103 us: solve_rows(): factor = jnp.linalg.cholesky(hadamard)]
    all_gather x4 -> x0, blocking collectives: 159 us -> none  [the longest x1 54.1 us: per_device(): block_c = lax.all_gather(factor_c, ('ia', 'ja'), axis=0, tiled=True)]
    psum x1 -> x0, blocking collectives: 74.6 us -> none  [per_device(): norms = lax.psum(jnp.sum(raw_c * raw_c, axis=0), ('ia', 'ja', 'ka'))]
    dot_general x7 -> x0, matrix products: 54.6 us -> none  [contract(): return jnp.einsum(form, left, right, precision=lax.Precision.HIGHEST)]
  transfers between devices with their start and end apart: 6 -> 0, of which waited for: 6 -> 0; matrix products, arithmetic and copies ran while one was open for 6% -> 0% of each run, Pallas kernels for 0% -> 0%
where the time goes in v1:
time: 172 us
  Pallas kernels  168 us (98%)
  local copies, waits for them, and re-layouts  3.13 us (2%)
    pallas_call x1, Pallas kernels, per_device(): pl.pallas_call(functools.partial(kernel, ni, nj, nk, counts), out_shape=(...  168 us

profile of v1, /device:TPU:1, one launch (start us, length us, event | category | flops | bytes accessed | tf_op | source)
XLA Modules:
  0.0 172.1 jit_solution(8151172025901631270)
XLA Ops:
  0.6 0.0 copy-start
  0.6 0.7 copy-done
  1.3 0.0 copy-start.1
  1.3 0.7 copy-done.1
  2.0 168.3 %shard_map.58 = (f32[4,256]{1,0:T(4,128)S(1)}, f32[4,256]{1,0:T(4,128)S(1)}, f32[2,256]{1,0:T(2,128)S(1)}) custom-call(f32[16384,128]{1,0:T(8,128)} %bitcast.1, f32[4,256]{1,0:T(4,128)S(1)} %copy-done, f32[2,256]{1,0:T(2,128)S(1)} %copy-done.1), custom_call_target="tpu_custom_call" | custom-call | tf_op jit(solution)/shard_map/pallas_call | solution.py:386
  170.4 0.6 copy.9
  170.9 0.6 copy.10
  171.5 0.6 copy.11
Async XLA Ops:
  0.6 0.7 copy-start
  1.3 0.7 copy-start.1

commit v2 on v1

v2 whole, which is shorter than its diff:
```python
import functools

import jax
import jax.numpy as jnp
from jax import lax
from jax.experimental import pallas as pl
from jax.experimental.pallas import tpu as pltpu
from jax.sharding import PartitionSpec as P

MESH = pl.DeviceIdType.MESH
F32 = jnp.float32
BF16 = jnp.bfloat16
HIGHEST = lax.Precision.HIGHEST
PIV = 32
GROUP = 8
SERVE = 4
SERVE_B = 4
SERVE_C = 3
TURNS = (32, 96)


def split(v):
    hi = v.astype(BF16)
    lo = (v - hi.astype(F32)).astype(BF16)
    return hi, lo


def stack_split(v):
    hi, lo = split(v)
    return jnp.concatenate([hi, hi], axis=0), jnp.concatenate([lo, lo], axis=0)


def mxu(left, right):
    return jnp.dot(left, right, preferred_element_type=F32)


def dot_full(left, right):
    return jnp.dot(left, right, preferred_element_type=F32, precision=HIGHEST)


def gram_of(rows):
    return lax.dot_general(
        rows, rows, (((0,), (0,)), ((), ())), preferred_element_type=F32, precision=HIGHEST
    )


def diagonals(matrix):
    n = matrix.shape[0]
    row = lax.broadcasted_iota(jnp.int32, (n, n), 0)
    col = lax.broadcasted_iota(jnp.int32, (n, n), 1)
    only = jnp.where(row == col, matrix, 0.0)
    return jnp.sum(only, axis=0, keepdims=True), jnp.sum(only, axis=1, keepdims=True)


def pivot_eight(rows, first):
    n = rows.shape[1]
    sub = lax.broadcasted_iota(jnp.int32, (8, 128), 0)
    lane = lax.broadcasted_iota(jnp.int32, (8, 128), 1)
    cols = [jnp.broadcast_to(rows[:, first + j : first + j + 1], (8, 128)) for j in range(8)]
    parts = [rows[:, h : h + 128] for h in range(0, n, 128)]
    for p in range(8):
        here = sub == p
        pivot = cols[p]
        inverse = 1.0 / jnp.broadcast_to(pivot[p : p + 1, :], (8, 128))
        parts[0] = jnp.where(lane == first + p, jnp.where(here, 1.0, 0.0), parts[0])

        def eliminate(v):
            scaled = jnp.broadcast_to(v[p : p + 1, :], (8, 128)) * inverse
            return jnp.where(here, scaled, v - pivot * scaled)

        parts = [eliminate(v) for v in parts]
        for j in range(p + 1, 8):
            cols[j] = eliminate(cols[j])
    return jnp.concatenate(parts, axis=1)


def pivot_panel(front):
    n = front.shape[1]
    groups = [front[g : g + 8, :] for g in range(0, PIV, 8)]
    lane = lax.broadcasted_iota(jnp.int32, (8, n), 1)
    for t in range(len(groups)):
        others = [g for g in range(len(groups)) if g != t]
        cols = {
            g: [jnp.broadcast_to(groups[g][:, 8 * t + j : 8 * t + j + 1], (8, n)) for j in range(8)]
            for g in others
        }
        groups[t] = pivot_eight(groups[t], 8 * t)
        wide = [jnp.broadcast_to(groups[t][j : j + 1, :], (8, n)) for j in range(8)]
        inside = (lane >= 8 * t) & (lane < 8 * t + 8)
        for g in others:
            terms = [cols[g][j] * wide[j] for j in range(8)]
            while len(terms) > 1:
                terms = [terms[i] + terms[i + 1] for i in range(0, len(terms), 2)]
            groups[g] = jnp.where(inside, 0.0, groups[g]) - terms[0]
    return jnp.concatenate(groups, axis=0)


def sweep_step(mat):
    n = mat.shape[0]
    front = mat[0:PIV, :]
    panel = pivot_panel(front)
    lane = lax.broadcasted_iota(jnp.int32, (PIV, n), 1)
    tall = jnp.concatenate([panel, jnp.zeros((128 - PIV, n), F32)], axis=0).T
    front_wide = jnp.concatenate([front, jnp.zeros((128 - PIV, n), F32)], axis=0)
    rest = mat[PIV:, :] - dot_full(tall[PIV:, :], front_wide)
    tall_wide = jnp.concatenate([tall[PIV:, :], jnp.zeros((n - PIV, n - 128), F32)], axis=1)
    rest_lane = lax.broadcasted_iota(jnp.int32, (n - PIV, n), 1)
    rest = jnp.where(rest_lane < PIV, tall_wide, rest)
    top = jnp.where(lane < PIV, -panel, panel)
    return pltpu.roll(jnp.concatenate([rest, top], axis=0), n - PIV, 1)


def invert_in(ref, first=0, last=None):
    def step(_, carry):
        ref[...] = sweep_step(ref[...])
        return carry

    lax.fori_loop(first, ref.shape[0] // PIV if last is None else last, step, 0)


def kernel(
    ni, nj, nk, counts,
    x_hbm, b_hbm, c_hbm, oa_ref, ob_ref, oc_ref,
    xs, xt, ys, bin_, cin, bblk, cblk, ablk, nblk, whi, wlo, rows, fac, arow,
    part_a, part_b, part_c, recv_a, recv_b, recv_c, own_a, own_b, own_c, gat_a, gat_b, gat_c,
    bx, cy, nx, half_b, half_c, half_n, other_b, other_c, other_n,
    gp_a, ex_a, sum_a, g_a, gcm, hmat, gca, nrm, own_n,
    ss, rs, xsem,
):
    rank = b_hbm.shape[1]
    nblkrows = 128
    ia, ja, ka = lax.axis_index("ia"), lax.axis_index("ja"), lax.axis_index("ka")
    n_a, n_b, n_c, nx_ = nj * nk, ni * nk, ni * nj, nj // 2
    me_a, me_b, me_c = ja * nk + ka, ia * nk + ka, ia * nj + ja
    x, core = ja // 2, lax.rem(ja, 2)

    def peer_a(q):
        return {"ia": ia, "ja": q // nk, "ka": lax.rem(q, nk)}

    def peer_b(q):
        return {"ia": q // nk, "ja": ja, "ka": lax.rem(q, nk)}

    def peer_c(q):
        return {"ia": q // nj, "ja": lax.rem(q, nj), "ka": ka}

    def line_i(q):
        return {"ia": q, "ja": ja, "ka": ka}

    def line_j(q):
        return {"ia": ia, "ja": q, "ka": ka}

    def line_k(q):
        return {"ia": ia, "ja": ja, "ka": q}

    started = []

    def line_x(q):
        return {"ia": ia, "ja": q * 2 + core, "ka": ka}

    def sibling(q):
        return {"ia": ia, "ja": x * 2 + q, "ka": ka}

    def send(phase, n, me, peer, src_of, dst, buf):
        started.append((phase, n, me, peer, buf))

        def go(p, carry):
            q = lax.rem(me + p, n)
            pltpu.make_async_remote_copy(
                src_ref=src_of(q), dst_ref=dst, send_sem=ss.at[phase], recv_sem=rs.at[phase],
                device_id=peer(q), device_id_type=MESH,
            ).start()
            return carry
        lax.fori_loop(1, n, go, 0)

    def all_of(phase, n, me, peer, buf):
        some = buf.at[pl.ds(0, n - 1)]
        return pltpu.make_async_remote_copy(
            src_ref=some, dst_ref=some, send_sem=ss.at[phase], recv_sem=rs.at[phase],
            device_id=peer(lax.rem(me + 1, n)), device_id_type=MESH,
        )

    def assemble(dst, src):
        per = src.shape[-2]
        count = dst.shape[0] // per
        inner = src.shape[1]
        for s in range(count):
            dst[s * per : (s + 1) * per, :] = src[s] if len(src.shape) == 3 else src[s // inner, s % inner]

    def scatter_out(dst, src):
        n, per = dst.shape[0], dst.shape[1]
        for s in range(n):
            dst[s] = src[s * per : (s + 1) * per, :]

    def own_rows(blk, me, per):
        if per >= 8:
            return blk[pl.ds(pl.multiple_of(me * per, 8), per), :]
        shared = 8 // per
        tile = blk[pl.ds(pl.multiple_of(me // shared * 8, 8), 8), :]
        mine = tile[0:per]
        for t in range(1, shared):
            mine = jnp.where(lax.rem(me, shared) == t, tile[t * per : (t + 1) * per], mine)
        return mine

    xcopy = pltpu.make_async_copy(x_hbm, xs, xsem.at[0])
    xcopy.start()
    bcopy = pltpu.make_async_copy(b_hbm, bin_.at[ia, ka], xsem.at[1])
    bcopy.start()
    ccopy = pltpu.make_async_copy(c_hbm, cin.at[ia, ja], xsem.at[2])
    ccopy.start()
    barrier = pltpu.get_barrier_semaphore()

    def hello(n, me, peer):
        def go(p, carry):
            pl.semaphore_signal(barrier, inc=1, device_id=peer(lax.rem(me + p, n)), device_id_type=MESH)
            return carry
        lax.fori_loop(1, n, go, 0)

    hello(ni, ia, line_i)
    hello(nj, ja, line_j)
    hello(nk, ka, line_k)

    def turn(j, carry):
        hi, lo = split(xs[pl.ds(j, nblkrows, stride=nblkrows), :].T)
        at = pl.ds(pl.multiple_of(j * nblkrows, nblkrows), nblkrows)
        xt[at, 0:128] = hi
        xt[at, 128:256] = lo
        return carry

    def turn_some(first, last):
        lax.fori_loop(first, last, turn, 0, unroll=4)

    bcopy.wait()
    ccopy.wait()
    xcopy.wait()
    turn_some(0, TURNS[0])
    pl.semaphore_wait(barrier, ni + nj + nk - 3)

    send(0, nk, ka, line_k, lambda q: bin_.at[ia, ka], bin_.at[ia, ka], bin_.at[ia])
    send(1, nj, ja, line_j, lambda q: cin.at[ia, ja], cin.at[ia, ja], cin.at[ia])
    turn_some(TURNS[0], TURNS[1])
    all_of(0, nk, ka, line_k, bin_.at[ia]).wait_recv()
    send(2, ni, ia, line_i, lambda q: bin_.at[ia], bin_.at[ia], bin_)
    all_of(1, nj, ja, line_j, cin.at[ia]).wait_recv()
    send(3, ni, ia, line_i, lambda q: cin.at[ia], cin.at[ia], cin)
    turn_some(TURNS[1], 128)
    all_of(2, ni, ia, line_i, bin_).wait_recv()
    assemble(bblk, bin_)
    bx[x] = bblk[...]
    send(4, nx_, x, line_x, lambda q: bblk, bx.at[x], bx)
    all_of(3, ni, ia, line_i, cin).wait_recv()
    assemble(cblk, cin)
    mine = pl.ds(pl.multiple_of(core * 64, 64), 64)
    cy[ka] = cblk[mine, :]
    send(5, nk, ka, line_k, lambda q: cblk.at[mine], cy.at[ka], cy)

    def gram_slices(dst, blk):
        dst[...] = gram_of(blk[...]).reshape(dst.shape)

    whi[...], wlo[...] = stack_split(cblk[...])
    step_rows = GROUP * nblkrows

    def mode_one(g, carry):
        at = pl.ds(pl.multiple_of(g * step_rows, step_rows), step_rows)
        hi, lo = split(xs[at, :])
        both = jnp.concatenate([hi, lo], axis=1)
        y = mxu(both, whi[...]) + mxu(both, wlo[...])
        ys[at, :] = y
        terms = y.reshape(GROUP, nblkrows, rank) * bblk[...][None]
        rows[pl.ds(pl.multiple_of(g * GROUP, GROUP), GROUP), :] = jnp.sum(terms, axis=1)
        return carry

    steps = 128 // GROUP
    lax.fori_loop(0, steps, mode_one, 0)

    scatter_out(part_a, rows)
    recv_a[me_a] = part_a[me_a]
    send(6, n_a, me_a, peer_a, lambda q: part_a.at[q], recv_a.at[me_a], recv_a)

    def swap(phase, half, other):
        send(phase, 2, core, sibling, lambda q: half, other.at[0], other)

    def swapped(phase, half, other):
        all_of(phase, 2, core, sibling, other).wait_recv()
        return half[...] + other[0]

    all_of(5, nk, ka, line_k, cy).wait_recv()
    half_c[...] = gram_of(cy[...].reshape(nk * 64, rank))
    swap(7, half_c, other_c)
    all_of(4, nx_, x, line_x, bx).wait_recv()
    half_b[...] = gram_of(bx[...].reshape(nx_ * 128, rank))
    swap(8, half_b, other_b)
    gcm[...] = swapped(7, half_c, other_c)
    hmat[...] = swapped(8, half_b, other_b) * gcm[...]
    invert_in(hmat, 0, SERVE)
    all_of(6, n_a, me_a, peer_a, recv_a).wait_recv()
    own_a[...] = jnp.sum(recv_a[...], axis=0)
    gat_a[me_a] = own_a[...]
    send(9, n_a, me_a, peer_a, lambda q: own_a, gat_a.at[me_a], gat_a)
    invert_in(hmat, SERVE)

    all_of(9, n_a, me_a, peer_a, gat_a).wait_recv()
    assemble(ablk, gat_a)
    ablk[...] = -dot_full(ablk[...], hmat[...])

    gram_slices(gp_a, ablk)
    ex_a[ia] = gp_a[me_a]
    send(10, ni, ia, line_i, lambda q: gp_a.at[me_a], ex_a.at[ia], ex_a)

    def sum_rows(factor):
        def add(s, total):
            at = pl.ds(pl.multiple_of(s * nblkrows, nblkrows), nblkrows)
            return total + ys[at, :] * factor[pl.ds(s, 1), :]
        return lax.fori_loop(0, 128, add, jnp.zeros((nblkrows, rank), F32), unroll=8)

    rows[...] = sum_rows(ablk)
    scatter_out(part_b, rows)
    recv_b[me_b] = part_b[me_b]
    send(12, n_b, me_b, peer_b, lambda q: part_b.at[q], recv_b.at[me_b], recv_b)

    whi[...], wlo[...] = stack_split(ablk[...])

    def third(g, carry):
        at = pl.ds(pl.multiple_of(g * step_rows, step_rows), step_rows)
        both = xt[at, :]
        ys[at, :] = mxu(both, whi[...]) + mxu(both, wlo[...])
        return carry
    lax.fori_loop(0, steps // 2, third, 0)
    all_of(10, ni, ia, line_i, ex_a).wait_recv()
    total_a = jnp.sum(ex_a[...], axis=0)
    sum_a[...] = total_a
    g_a[me_a] = total_a
    send(11, n_a, me_a, peer_a, lambda q: sum_a, g_a.at[me_a], g_a)

    lax.fori_loop(steps // 2, steps, third, 0)

    all_of(12, n_b, me_b, peer_b, recv_b).wait_recv()
    own_b[...] = jnp.sum(recv_b[...], axis=0)
    gat_b[me_b] = own_b[...]
    send(13, n_b, me_b, peer_b, lambda q: own_b, gat_b.at[me_b], gat_b)

    all_of(11, n_a, me_a, peer_a, g_a).wait_recv()
    gram = g_a[...].reshape(rank, rank)
    along, down = diagonals(gram)
    scale_a = jnp.sqrt(along / counts[0] + 1e-06)
    inverse_a = 1.0 / scale_a
    gca[...] = (gram * inverse_a) * (1.0 / jnp.sqrt(down / counts[0] + 1e-06))
    hmat[...] = gca[...] * gcm[...]
    oa_ref[...] = own_rows(ablk, me_a, oa_ref.shape[0]) / scale_a
    arow[...] = inverse_a
    invert_in(hmat, 0, SERVE_B)
    all_of(13, n_b, me_b, peer_b, gat_b).wait_recv()
    assemble(nblk, gat_b)
    nx[x] = nblk[...]
    send(14, nx_, x, line_x, lambda q: nblk, nx.at[x], nx)
    invert_in(hmat, SERVE_B)
    raw_b = -dot_full(nblk[...] * arow[...], hmat[...])
    ablk[...] = raw_b

    fac[...] = raw_b * arow[...]
    rows[...] = sum_rows(fac)
    scatter_out(part_c, rows)
    recv_c[me_c] = part_c[me_c]
    send(15, n_c, me_c, peer_c, lambda q: part_c.at[q], recv_c.at[me_c], recv_c)

    all_of(14, nx_, x, line_x, nx).wait_recv()
    half_n[...] = gram_of(-dot_full(nx[...].reshape(nx_ * 128, rank) * arow[...], hmat[...]))
    swap(16, half_n, other_n)
    gram = swapped(16, half_n, other_n)
    along, down = diagonals(gram)
    scale_b = jnp.sqrt(along / counts[1] + 1e-06)
    inverse_b = 1.0 / scale_b
    hmat[...] = gca[...] * ((gram * inverse_b) * (1.0 / jnp.sqrt(down / counts[1] + 1e-06)))
    ob_ref[...] = own_rows(ablk, me_b, ob_ref.shape[0]) / scale_b
    arow[...] = inverse_b
    invert_in(hmat, 0, SERVE_C)
    all_of(15, n_c, me_c, peer_c, recv_c).wait_recv()
    own_c[...] = jnp.sum(recv_c[...], axis=0)
    gat_c[ia] = own_c[...]
    send(17, ni, ia, line_i, lambda q: own_c, gat_c.at[ia], gat_c)
    invert_in(hmat, SERVE_C)

    all_of(17, ni, ia, line_i, gat_c).wait_recv()
    per = own_c.shape[0]
    assemble(fac.at[pl.ds(0, ni * per)], gat_c)
    raw_c = -dot_full(fac[0 : ni * per, :] * arow[...], hmat[...])
    squares = jnp.sum(raw_c * raw_c, axis=0, keepdims=True)
    own_n[...] = squares
    nrm[me_a] = squares
    send(18, n_a, me_a, peer_a, lambda q: own_n, nrm.at[me_a], nrm)
    mine_c = raw_c[0:per]
    for t in range(1, ni):
        mine_c = jnp.where(ia == t, raw_c[t * per : (t + 1) * per], mine_c)
    all_of(18, n_a, me_a, peer_a, nrm).wait_recv()
    squares = jnp.sum(nrm[...], axis=0)
    oc_ref[...] = mine_c / jnp.sqrt(squares / counts[2] + 1e-06)

    for phase, n, me, peer, buf in started:
        all_of(phase, n, me, peer, buf).wait_send()


def per_device(ni, nj, nk, tensor, factor_b, factor_c):
    counts = (tensor.shape[0] * ni, tensor.shape[1] * nj, tensor.shape[2] * nk)
    rank = factor_b.shape[1]
    n_a, n_b, n_c, n_x = nj * nk, ni * nk, ni * nj, nj // 2
    r_a, r_b, r_c = 128 // n_a, 128 // n_b, 128 // n_c
    v = lambda *shape: pltpu.VMEM(shape, F32)
    square = v(rank, rank)
    scratch = [
        v(16384, 128), pltpu.VMEM((16384, 256), BF16), v(16384, rank),
        v(ni, nk, r_b, rank), v(ni, nj, r_c, rank),
        v(128, rank), v(128, rank), v(128, rank), v(128, rank),
        pltpu.VMEM((256, rank), BF16), pltpu.VMEM((256, rank), BF16),
        v(128, rank), v(128, rank), v(1, rank),
        v(n_a, r_a, rank), v(n_b, r_b, rank), v(n_c, r_c, rank),
        v(n_a, r_a, rank), v(n_b, r_b, rank), v(n_c, r_c, rank),
        v(r_a, rank), v(r_b, rank), v(r_c, rank),
        v(n_a, r_a, rank), v(n_b, r_b, rank), v(ni, r_c, rank),
        v(n_x, 128, rank), v(nk, 64, rank), v(n_x, 128, rank),
        square, square, square, v(1, rank, rank), v(1, rank, rank), v(1, rank, rank),
        v(n_a, rank // n_a, rank), v(ni, rank // n_a, rank), v(rank // n_a, rank), v(n_a, rank // n_a, rank),
        square, square, square, v(n_a, 1, rank), v(1, rank),
        pltpu.SemaphoreType.DMA((19,)), pltpu.SemaphoreType.DMA((19,)), pltpu.SemaphoreType.DMA((3,)),
    ]
    vmem = pl.BlockSpec(memory_space=pltpu.VMEM)
    return pl.pallas_call(
        functools.partial(kernel, ni, nj, nk, counts),
        out_shape=(
            jax.ShapeDtypeStruct((r_a, rank), F32),
            jax.ShapeDtypeStruct((r_b, rank), F32),
            jax.ShapeDtypeStruct((r_c, rank), F32),
        ),
        in_specs=[pl.BlockSpec(memory_space=pl.ANY)] * 3,
        out_specs=(vmem, vmem, vmem),
        scratch_shapes=scratch,
        compiler_params=pltpu.CompilerParams(
            collective_id=0, has_side_effects=True, vmem_limit_bytes=52 * 1024 * 1024
        ),
    )(tensor.reshape(16384, 128), factor_b, factor_c)


def solution(mesh):
    ni, nj, nk = mesh.shape["ia"], mesh.shape["ja"], mesh.shape["ka"]
    return jax.shard_map(
        functools.partial(per_device, ni, nj, nk),
        mesh=mesh,
        in_specs=(P("ia", "ja", "ka"), P(("ja", "ia", "ka"), None), P(("ka", "ia", "ja"), None)),
        out_specs=(
            P(("ia", "ja", "ka"), None),
            P(("ja", "ia", "ka"), None),
            P(("ka", "ia", "ja"), None),
        ),
        check_vma=False,
    )
```

time: 172 us -> 100 us (0.58)
  Pallas kernels: 168 us -> 96.4 us
    pallas_call x1, Pallas kernels: 168 us -> 96.4 us  [per_device(): pl.pallas_call(functools.partial(kernel, ni, nj, nk, counts), out_shape=(...]
where the time goes in v2:
time: 100 us
  Pallas kernels  96.4 us (96%)
  local copies, waits for them, and re-layouts  3.13 us (3%)
    pallas_call x1, Pallas kernels, per_device(): pl.pallas_call(functools.partial(kernel, ni, nj, nk, counts), out_shape=(...  96.4 us
    unnamed x7, local copies, waits for them, and re-layouts  3.13 us

profile of v2, /device:TPU:1, one launch (start us, length us, event | category | flops | bytes accessed | tf_op | source)
XLA Modules:
  0.0 100.2 jit_solution(2457202031383934214)
XLA Ops:
  0.6 0.0 copy-start
  0.6 0.7 copy-done
  1.3 0.0 copy-start.1
  1.3 0.7 copy-done.1
  2.0 96.4 %shard_map.58 = (f32[4,256]{1,0:T(4,128)S(1)}, f32[4,256]{1,0:T(4,128)S(1)}, f32[2,256]{1,0:T(2,128)S(1)}) custom-call(f32[16384,128]{1,0:T(8,128)} %bitcast.1, f32[4,256]{1,0:T(4,128)S(1)} %copy-done, f32[2,256]{1,0:T(2,128)S(1)} %copy-done.1), custom_call_target="tpu_custom_call" | custom-call | tf_op jit(solution)/shard_map/pallas_call | solution.py:425
  98.4 0.6 copy.9
  99.0 0.6 copy.10
  99.6 0.6 copy.11
Async XLA Ops:
  0.6 0.7 copy-start
  1.3 0.7 copy-start.1

commit v3 on v2

--- a/solution.py
+++ b/solution.py
@@ -11,12 +11,13 @@
 F32 = jnp.float32
 BF16 = jnp.bfloat16
 HIGHEST = lax.Precision.HIGHEST
-PIV = 32
-GROUP = 8
-SERVE = 4
-SERVE_B = 4
-SERVE_C = 3
-TURNS = (32, 96)
+PIV = 64
+BLOCK = 16
+GROUP = 32
+SERVE = 2
+SERVE_B = 2
+SERVE_C = 1
+TURNS = (48, 96)
 
 
 def split(v):
@@ -52,60 +53,86 @@
     return jnp.sum(only, axis=0, keepdims=True), jnp.sum(only, axis=1, keepdims=True)
 
 
-def pivot_eight(rows, first):
-    n = rows.shape[1]
+def row_of(v, r):
+    return jnp.broadcast_to(v[r : r + 1, :], v.shape)
+
+
+def pivot_block(groups, first):
+    n = groups[0].shape[1]
     sub = lax.broadcasted_iota(jnp.int32, (8, 128), 0)
     lane = lax.broadcasted_iota(jnp.int32, (8, 128), 1)
-    cols = [jnp.broadcast_to(rows[:, first + j : first + j + 1], (8, 128)) for j in range(8)]
-    parts = [rows[:, h : h + 128] for h in range(0, n, 128)]
-    for p in range(8):
-        here = sub == p
-        pivot = cols[p]
-        inverse = 1.0 / jnp.broadcast_to(pivot[p : p + 1, :], (8, 128))
-        parts[0] = jnp.where(lane == first + p, jnp.where(here, 1.0, 0.0), parts[0])
-
-        def eliminate(v):
-            scaled = jnp.broadcast_to(v[p : p + 1, :], (8, 128)) * inverse
-            return jnp.where(here, scaled, v - pivot * scaled)
-
-        parts = [eliminate(v) for v in parts]
-        for j in range(p + 1, 8):
+    cols = [[jnp.broadcast_to(g[:, first + j : first + j + 1], (8, 128)) for g in groups] for j in range(BLOCK)]
+    parts = [[g[:, h : h + 128] for g in groups] for h in range(0, n, 128)]
+    for p in range(BLOCK):
+        group, r = p // 8, p % 8
+        here = sub == r
+        inverse = 1.0 / row_of(cols[p][group], r)
+        factor = [v * inverse for v in cols[p]]
+        factor[group] = jnp.where(here, 1.0 - inverse, factor[group])
+        parts[0] = [
+            jnp.where(lane == first + p, jnp.where(here, 1.0, 0.0) if g == group else 0.0, v)
+            for g, v in enumerate(parts[0])
+        ]
+
+        def eliminate(vs):
+            row = row_of(vs[group], r)
+            return [v - f * row for v, f in zip(vs, factor)]
+
+        for j in range(p + 1, BLOCK):
             cols[j] = eliminate(cols[j])
-    return jnp.concatenate(parts, axis=1)
+        parts = [eliminate(vs) for vs in parts]
+    return [jnp.concatenate(vs, axis=1) for vs in zip(*parts)]
 
 
 def pivot_panel(front):
     n = front.shape[1]
+    size = BLOCK // 8
     groups = [front[g : g + 8, :] for g in range(0, PIV, 8)]
     lane = lax.broadcasted_iota(jnp.int32, (8, n), 1)
-    for t in range(len(groups)):
-        others = [g for g in range(len(groups)) if g != t]
+    blocks = PIV // BLOCK
+    for t in range(blocks):
+        own = list(range(t * size, t * size + size))
+        others = [g for g in range(len(groups)) if g not in own]
+        near = others if t == blocks - 1 else [g for g in others if own[-1] < g <= own[-1] + size]
+        far = [g for g in others if g not in near]
+        first = t * BLOCK
         cols = {
-            g: [jnp.broadcast_to(groups[g][:, 8 * t + j : 8 * t + j + 1], (8, n)) for j in range(8)]
-            for g in others
+            g: [jnp.broadcast_to(groups[g][:, first + j : first + j + 1], (8, 128)) for j in range(BLOCK)]
+            for g in near
         }
-        groups[t] = pivot_eight(groups[t], 8 * t)
-        wide = [jnp.broadcast_to(groups[t][j : j + 1, :], (8, n)) for j in range(8)]
-        inside = (lane >= 8 * t) & (lane < 8 * t + 8)
-        for g in others:
-            terms = [cols[g][j] * wide[j] for j in range(8)]
-            while len(terms) > 1:
-                terms = [terms[i] + terms[i + 1] for i in range(0, len(terms), 2)]
-            groups[g] = jnp.where(inside, 0.0, groups[g]) - terms[0]
+        new = pivot_block([groups[g] for g in own], first)
+        wide = [row_of(new[j // 8], j % 8) for j in range(BLOCK)]
+        inside = (lane >= first) & (lane < first + BLOCK)
+        before = list(groups)
+        for g, v in zip(own, new):
+            groups[g] = v
+        for g in near:
+            halves = []
+            for h in range(0, n, 128):
+                terms = [cols[g][j] * wide[j][:, h : h + 128] for j in range(BLOCK)]
+                while len(terms) > 1:
+                    terms = [terms[i] + terms[i + 1] for i in range(0, len(terms), 2)]
+                halves.append(terms[0])
+            groups[g] = jnp.where(inside, 0.0, before[g]) - jnp.concatenate(halves, axis=1)
+        if far:
+            left = jnp.concatenate([jnp.where(inside, before[g], 0.0)[:, 0:128] for g in far], axis=0)
+            right = ([jnp.zeros((first, n), F32)] if first else []) + new + [jnp.zeros((128 - first - BLOCK, n), F32)]
+            product = dot_full(left, jnp.concatenate(right, axis=0))
+            for i, g in enumerate(far):
+                groups[g] = jnp.where(inside, 0.0, before[g]) - product[8 * i : 8 * i + 8, :]
     return jnp.concatenate(groups, axis=0)
 
 
 def sweep_step(mat):
     n = mat.shape[0]
-    front = mat[0:PIV, :]
-    panel = pivot_panel(front)
+    panel = pivot_panel(mat[0:PIV, :])
     lane = lax.broadcasted_iota(jnp.int32, (PIV, n), 1)
-    tall = jnp.concatenate([panel, jnp.zeros((128 - PIV, n), F32)], axis=0).T
-    front_wide = jnp.concatenate([front, jnp.zeros((128 - PIV, n), F32)], axis=0)
-    rest = mat[PIV:, :] - dot_full(tall[PIV:, :], front_wide)
-    tall_wide = jnp.concatenate([tall[PIV:, :], jnp.zeros((n - PIV, n - 128), F32)], axis=1)
     rest_lane = lax.broadcasted_iota(jnp.int32, (n - PIV, n), 1)
-    rest = jnp.where(rest_lane < PIV, tall_wide, rest)
+    panel_wide = jnp.concatenate([panel, jnp.zeros((128 - PIV, n), F32)], axis=0)
+    left = jnp.where(rest_lane[:, 0:128] < PIV, mat[PIV:, 0:128], 0.0)
+    rest = mat[PIV:, :] - dot_full(left, panel_wide)
+    tall = jnp.concatenate([panel_wide.T[PIV:, :], jnp.zeros((n - PIV, n - 128), F32)], axis=1)
+    rest = jnp.where(rest_lane < PIV, tall, rest)
     top = jnp.where(lane < PIV, -panel, panel)
     return pltpu.roll(jnp.concatenate([rest, top], axis=0), n - PIV, 1)
 
@@ -118,10 +145,16 @@
     lax.fori_loop(first, ref.shape[0] // PIV if last is None else last, step, 0)
 
 
+def unit_diagonal(matrix):
+    along, down = diagonals(matrix)
+    along, down = 1.0 / jnp.sqrt(along), 1.0 / jnp.sqrt(down)
+    return (matrix * along) * down, along
+
+
 def kernel(
     ni, nj, nk, counts,
     x_hbm, b_hbm, c_hbm, oa_ref, ob_ref, oc_ref,
-    xs, xt, ys, bin_, cin, bblk, cblk, ablk, nblk, whi, wlo, rows, fac, arow,
+    xs, xt, ys, bin_, cin, bblk, cblk, ablk, nblk, whi, wlo, rows, fac, arow, hrow,
     part_a, part_b, part_c, recv_a, recv_b, recv_c, own_a, own_b, own_c, gat_a, gat_b, gat_c,
     bx, cy, nx, half_b, half_c, half_n, other_b, other_c, other_n,
     gp_a, ex_a, sum_a, g_a, gcm, hmat, gca, nrm, own_n,
@@ -182,9 +215,9 @@
     def assemble(dst, src):
         per = src.shape[-2]
         count = dst.shape[0] // per
-        inner = src.shape[1]
+        outer = src.shape[0]
         for s in range(count):
-            dst[s * per : (s + 1) * per, :] = src[s] if len(src.shape) == 3 else src[s // inner, s % inner]
+            dst[s * per : (s + 1) * per, :] = src[s] if len(src.shape) == 3 else src[s % outer, s // outer]
 
     def scatter_out(dst, src):
         n, per = dst.shape[0], dst.shape[1]
@@ -201,11 +234,14 @@
             mine = jnp.where(lax.rem(me, shared) == t, tile[t * per : (t + 1) * per], mine)
         return mine
 
+    def solve(summed):
+        return dot_full(summed * hrow[...], hmat[...]) * -hrow[...]
+
     xcopy = pltpu.make_async_copy(x_hbm, xs, xsem.at[0])
     xcopy.start()
-    bcopy = pltpu.make_async_copy(b_hbm, bin_.at[ia, ka], xsem.at[1])
+    bcopy = pltpu.make_async_copy(b_hbm, bin_.at[ka, ia], xsem.at[1])
     bcopy.start()
-    ccopy = pltpu.make_async_copy(c_hbm, cin.at[ia, ja], xsem.at[2])
+    ccopy = pltpu.make_async_copy(c_hbm, cin.at[ja, ia], xsem.at[2])
     ccopy.start()
     barrier = pltpu.get_barrier_semaphore()
 
@@ -227,7 +263,7 @@
         return carry
 
     def turn_some(first, last):
-        lax.fori_loop(first, last, turn, 0, unroll=4)
+        lax.fori_loop(first, last, turn, 0, unroll=16)
 
     bcopy.wait()
     ccopy.wait()
@@ -235,19 +271,19 @@
     turn_some(0, TURNS[0])
     pl.semaphore_wait(barrier, ni + nj + nk - 3)
 
-    send(0, nk, ka, line_k, lambda q: bin_.at[ia, ka], bin_.at[ia, ka], bin_.at[ia])
-    send(1, nj, ja, line_j, lambda q: cin.at[ia, ja], cin.at[ia, ja], cin.at[ia])
+    send(0, ni, ia, line_i, lambda q: bin_.at[ka, ia], bin_.at[ka, ia], bin_.at[ka])
+    send(1, ni, ia, line_i, lambda q: cin.at[ja, ia], cin.at[ja, ia], cin.at[ja])
     turn_some(TURNS[0], TURNS[1])
-    all_of(0, nk, ka, line_k, bin_.at[ia]).wait_recv()
-    send(2, ni, ia, line_i, lambda q: bin_.at[ia], bin_.at[ia], bin_)
-    all_of(1, nj, ja, line_j, cin.at[ia]).wait_recv()
-    send(3, ni, ia, line_i, lambda q: cin.at[ia], cin.at[ia], cin)
+    all_of(0, ni, ia, line_i, bin_.at[ka]).wait_recv()
+    send(2, nk, ka, line_k, lambda q: bin_.at[ka], bin_.at[ka], bin_)
+    all_of(1, ni, ia, line_i, cin.at[ja]).wait_recv()
+    send(3, nj, ja, line_j, lambda q: cin.at[ja], cin.at[ja], cin)
     turn_some(TURNS[1], 128)
-    all_of(2, ni, ia, line_i, bin_).wait_recv()
+    all_of(2, nk, ka, line_k, bin_).wait_recv()
     assemble(bblk, bin_)
     bx[x] = bblk[...]
     send(4, nx_, x, line_x, lambda q: bblk, bx.at[x], bx)
-    all_of(3, ni, ia, line_i, cin).wait_recv()
+    all_of(3, nj, ja, line_j, cin).wait_recv()
     assemble(cblk, cin)
     mine = pl.ds(pl.multiple_of(core * 64, 64), 64)
     cy[ka] = cblk[mine, :]
@@ -290,7 +326,7 @@
     half_b[...] = gram_of(bx[...].reshape(nx_ * 128, rank))
     swap(8, half_b, other_b)
     gcm[...] = swapped(7, half_c, other_c)
-    hmat[...] = swapped(8, half_b, other_b) * gcm[...]
+    hmat[...], hrow[...] = unit_diagonal(swapped(8, half_b, other_b) * gcm[...])
     invert_in(hmat, 0, SERVE)
     all_of(6, n_a, me_a, peer_a, recv_a).wait_recv()
     own_a[...] = jnp.sum(recv_a[...], axis=0)
@@ -300,11 +336,7 @@
 
     all_of(9, n_a, me_a, peer_a, gat_a).wait_recv()
     assemble(ablk, gat_a)
-    ablk[...] = -dot_full(ablk[...], hmat[...])
-
-    gram_slices(gp_a, ablk)
-    ex_a[ia] = gp_a[me_a]
-    send(10, ni, ia, line_i, lambda q: gp_a.at[me_a], ex_a.at[ia], ex_a)
+    ablk[...] = solve(ablk[...])
 
     def sum_rows(factor):
         def add(s, total):
@@ -316,6 +348,10 @@
     scatter_out(part_b, rows)
     recv_b[me_b] = part_b[me_b]
     send(12, n_b, me_b, peer_b, lambda q: part_b.at[q], recv_b.at[me_b], recv_b)
+
+    gram_slices(gp_a, ablk)
+    ex_a[ia] = gp_a[me_a]
+    send(10, ni, ia, line_i, lambda q: gp_a.at[me_a], ex_a.at[ia], ex_a)
 
     whi[...], wlo[...] = stack_split(ablk[...])
 
@@ -344,7 +380,7 @@
     scale_a = jnp.sqrt(along / counts[0] + 1e-06)
     inverse_a = 1.0 / scale_a
     gca[...] = (gram * inverse_a) * (1.0 / jnp.sqrt(down / counts[0] + 1e-06))
-    hmat[...] = gca[...] * gcm[...]
+    hmat[...], hrow[...] = unit_diagonal(gca[...] * gcm[...])
     oa_ref[...] = own_rows(ablk, me_a, oa_ref.shape[0]) / scale_a
     arow[...] = inverse_a
     invert_in(hmat, 0, SERVE_B)
@@ -353,7 +389,7 @@
     nx[x] = nblk[...]
     send(14, nx_, x, line_x, lambda q: nblk, nx.at[x], nx)
     invert_in(hmat, SERVE_B)
-    raw_b = -dot_full(nblk[...] * arow[...], hmat[...])
+    raw_b = solve(nblk[...] * arow[...])
     ablk[...] = raw_b
 
     fac[...] = raw_b * arow[...]
@@ -363,13 +399,13 @@
     send(15, n_c, me_c, peer_c, lambda q: part_c.at[q], recv_c.at[me_c], recv_c)
 
     all_of(14, nx_, x, line_x, nx).wait_recv()
-    half_n[...] = gram_of(-dot_full(nx[...].reshape(nx_ * 128, rank) * arow[...], hmat[...]))
+    half_n[...] = gram_of(solve(nx[...].reshape(nx_ * 128, rank) * arow[...]))
     swap(16, half_n, other_n)
     gram = swapped(16, half_n, other_n)
     along, down = diagonals(gram)
     scale_b = jnp.sqrt(along / counts[1] + 1e-06)
     inverse_b = 1.0 / scale_b
-    hmat[...] = gca[...] * ((gram * inverse_b) * (1.0 / jnp.sqrt(down / counts[1] + 1e-06)))
+    hmat[...], hrow[...] = unit_diagonal(gca[...] * ((gram * inverse_b) * (1.0 / jnp.sqrt(down / counts[1] + 1e-06))))
     ob_ref[...] = own_rows(ablk, me_b, ob_ref.shape[0]) / scale_b
     arow[...] = inverse_b
     invert_in(hmat, 0, SERVE_C)
@@ -382,7 +418,7 @@
     all_of(17, ni, ia, line_i, gat_c).wait_recv()
     per = own_c.shape[0]
     assemble(fac.at[pl.ds(0, ni * per)], gat_c)
-    raw_c = -dot_full(fac[0 : ni * per, :] * arow[...], hmat[...])
+    raw_c = solve(fac[0 : ni * per, :] * arow[...])
     squares = jnp.sum(raw_c * raw_c, axis=0, keepdims=True)
     own_n[...] = squares
     nrm[me_a] = squares
@@ -407,10 +443,10 @@
     square = v(rank, rank)
     scratch = [
         v(16384, 128), pltpu.VMEM((16384, 256), BF16), v(16384, rank),
-        v(ni, nk, r_b, rank), v(ni, nj, r_c, rank),
+        v(nk, ni, r_b, rank), v(nj, ni, r_c, rank),
         v(128, rank), v(128, rank), v(128, rank), v(128, rank),
         pltpu.VMEM((256, rank), BF16), pltpu.VMEM((256, rank), BF16),
-        v(128, rank), v(128, rank), v(1, rank),
+        v(128, rank), v(128, rank), v(1, rank), v(1, rank),
         v(n_a, r_a, rank), v(n_b, r_b, rank), v(n_c, r_c, rank),
         v(n_a, r_a, rank), v(n_b, r_b, rank), v(n_c, r_c, rank),
         v(r_a, rank), v(r_b, rank), v(r_c, rank),

time: 100 us -> 87.8 us (0.88)
  Pallas kernels: 96.4 us -> 83.9 us
    pallas_call x1, Pallas kernels: 96.4 us -> 83.9 us  [per_device(): pl.pallas_call(functools.partial(kernel, ni, nj, nk, counts), out_shape=(...]
where the time goes in v3:
time: 87.8 us; the launch traced here: 87.6 us
  Pallas kernels  83.9 us (96%)
  local copies, waits for them, and re-layouts  3.13 us (4%)
    pallas_call x1, Pallas kernels, per_device(): pl.pallas_call(functools.partial(kernel, ni, nj, nk, counts), out_shape=(...  83.9 us
    unnamed x7, local copies, waits for them, and re-layouts  3.13 us

profile of v3, /device:TPU:1, one launch (start us, length us, event | category | flops | bytes accessed | tf_op | source)
XLA Modules:
  0.0 87.6 jit_solution(15336296555422101462)
XLA Ops:
  0.6 0.0 copy-start
  0.6 0.7 copy-done
  1.3 0.0 copy-start.1
  1.3 0.7 copy-done.1
  2.0 83.9 %shard_map.58 = (f32[4,256]{1,0:T(4,128)S(1)}, f32[4,256]{1,0:T(4,128)S(1)}, f32[2,256]{1,0:T(2,128)S(1)}) custom-call(f32[16384,128]{1,0:T(8,128)} %bitcast.1, f32[4,256]{1,0:T(4,128)S(1)} %copy-done, f32[2,256]{1,0:T(2,128)S(1)} %copy-done.1), custom_call_target="tpu_custom_call" | custom-call | tf_op jit(solution)/shard_map/pallas_call | solution.py:461
  85.9 0.6 copy.9
  86.5 0.6 copy.10
  87.1 0.6 copy.11
Async XLA Ops:
  0.6 0.7 copy-start
  1.3 0.7 copy-start.1

commit v4 on v3

--- a/solution.py
+++ b/solution.py
@@ -17,7 +17,7 @@
 SERVE = 2
 SERVE_B = 2
 SERVE_C = 1
-TURNS = (48, 96)
+TURNS = 80
 
 
 def split(v):
@@ -153,7 +153,7 @@
 
 def kernel(
     ni, nj, nk, counts,
-    x_hbm, b_hbm, c_hbm, oa_ref, ob_ref, oc_ref,
+    x_hbm, b_hbm, c_hbm, out_ref,
     xs, xt, ys, bin_, cin, bblk, cblk, ablk, nblk, whi, wlo, rows, fac, arow, hrow,
     part_a, part_b, part_c, recv_a, recv_b, recv_c, own_a, own_b, own_c, gat_a, gat_b, gat_c,
     bx, cy, nx, half_b, half_c, half_n, other_b, other_c, other_n,
@@ -267,18 +267,17 @@
 
     bcopy.wait()
     ccopy.wait()
-    xcopy.wait()
-    turn_some(0, TURNS[0])
     pl.semaphore_wait(barrier, ni + nj + nk - 3)
 
     send(0, ni, ia, line_i, lambda q: bin_.at[ka, ia], bin_.at[ka, ia], bin_.at[ka])
     send(1, ni, ia, line_i, lambda q: cin.at[ja, ia], cin.at[ja, ia], cin.at[ja])
-    turn_some(TURNS[0], TURNS[1])
+    xcopy.wait()
+    turn_some(0, TURNS)
     all_of(0, ni, ia, line_i, bin_.at[ka]).wait_recv()
     send(2, nk, ka, line_k, lambda q: bin_.at[ka], bin_.at[ka], bin_)
     all_of(1, ni, ia, line_i, cin.at[ja]).wait_recv()
     send(3, nj, ja, line_j, lambda q: cin.at[ja], cin.at[ja], cin)
-    turn_some(TURNS[1], 128)
+    turn_some(TURNS, 128)
     all_of(2, nk, ka, line_k, bin_).wait_recv()
     assemble(bblk, bin_)
     bx[x] = bblk[...]
@@ -338,6 +337,10 @@
     assemble(ablk, gat_a)
     ablk[...] = solve(ablk[...])
 
+    gram_slices(gp_a, ablk)
+    ex_a[ia] = gp_a[me_a]
+    send(10, ni, ia, line_i, lambda q: gp_a.at[me_a], ex_a.at[ia], ex_a)
+
     def sum_rows(factor):
         def add(s, total):
             at = pl.ds(pl.multiple_of(s * nblkrows, nblkrows), nblkrows)
@@ -348,10 +351,6 @@
     scatter_out(part_b, rows)
     recv_b[me_b] = part_b[me_b]
     send(12, n_b, me_b, peer_b, lambda q: part_b.at[q], recv_b.at[me_b], recv_b)
-
-    gram_slices(gp_a, ablk)
-    ex_a[ia] = gp_a[me_a]
-    send(10, ni, ia, line_i, lambda q: gp_a.at[me_a], ex_a.at[ia], ex_a)
 
     whi[...], wlo[...] = stack_split(ablk[...])
 
@@ -381,7 +380,8 @@
     inverse_a = 1.0 / scale_a
     gca[...] = (gram * inverse_a) * (1.0 / jnp.sqrt(down / counts[0] + 1e-06))
     hmat[...], hrow[...] = unit_diagonal(gca[...] * gcm[...])
-    oa_ref[...] = own_rows(ablk, me_a, oa_ref.shape[0]) / scale_a
+    r_a, r_b, r_c = own_a.shape[0], own_b.shape[0], own_c.shape[0]
+    out_ref[0:r_a, :] = own_rows(ablk, me_a, r_a) / scale_a
     arow[...] = inverse_a
     invert_in(hmat, 0, SERVE_B)
     all_of(13, n_b, me_b, peer_b, gat_b).wait_recv()
@@ -406,7 +406,7 @@
     scale_b = jnp.sqrt(along / counts[1] + 1e-06)
     inverse_b = 1.0 / scale_b
     hmat[...], hrow[...] = unit_diagonal(gca[...] * ((gram * inverse_b) * (1.0 / jnp.sqrt(down / counts[1] + 1e-06))))
-    ob_ref[...] = own_rows(ablk, me_b, ob_ref.shape[0]) / scale_b
+    out_ref[r_a : r_a + r_b, :] = own_rows(ablk, me_b, r_b) / scale_b
     arow[...] = inverse_b
     invert_in(hmat, 0, SERVE_C)
     all_of(15, n_c, me_c, peer_c, recv_c).wait_recv()
@@ -428,10 +428,17 @@
         mine_c = jnp.where(ia == t, raw_c[t * per : (t + 1) * per], mine_c)
     all_of(18, n_a, me_a, peer_a, nrm).wait_recv()
     squares = jnp.sum(nrm[...], axis=0)
-    oc_ref[...] = mine_c / jnp.sqrt(squares / counts[2] + 1e-06)
+    out_ref[r_a + r_b : r_a + r_b + r_c, :] = mine_c / jnp.sqrt(squares / counts[2] + 1e-06)
 
     for phase, n, me, peer, buf in started:
         all_of(phase, n, me, peer, buf).wait_send()
+
+
+def part_outputs(in_ref, *out_refs):
+    first = 0
+    for ref in out_refs:
+        ref[...] = in_ref[first : first + ref.shape[0], :]
+        first += ref.shape[0]
 
 
 def per_device(ni, nj, nk, tensor, factor_b, factor_c):
@@ -458,20 +465,22 @@
         pltpu.SemaphoreType.DMA((19,)), pltpu.SemaphoreType.DMA((19,)), pltpu.SemaphoreType.DMA((3,)),
     ]
     vmem = pl.BlockSpec(memory_space=pltpu.VMEM)
-    return pl.pallas_call(
+    stacked = pl.pallas_call(
         functools.partial(kernel, ni, nj, nk, counts),
-        out_shape=(
-            jax.ShapeDtypeStruct((r_a, rank), F32),
-            jax.ShapeDtypeStruct((r_b, rank), F32),
-            jax.ShapeDtypeStruct((r_c, rank), F32),
-        ),
+        out_shape=jax.ShapeDtypeStruct((r_a + r_b + r_c, rank), F32),
         in_specs=[pl.BlockSpec(memory_space=pl.ANY)] * 3,
-        out_specs=(vmem, vmem, vmem),
+        out_specs=vmem,
         scratch_shapes=scratch,
         compiler_params=pltpu.CompilerParams(
-            collective_id=0, has_side_effects=True, vmem_limit_bytes=52 * 1024 * 1024
+            collective_id=0, has_side_effects=True, vmem_limit_bytes=60 * 1024 * 1024
         ),
     )(tensor.reshape(16384, 128), factor_b, factor_c)
+    return pl.pallas_call(
+        part_outputs,
+        out_shape=tuple(jax.ShapeDtypeStruct((r, rank), F32) for r in (r_a, r_b, r_c)),
+        in_specs=[vmem],
+        out_specs=(vmem, vmem, vmem),
+    )(stacked)
 
 
 def solution(mesh):

time: 87.8 us -> 80.9 us (0.921)
  Pallas kernels: 83.9 us -> 80.1 us
  local copies, waits for them, and re-layouts: 3.13 us -> 0 us
    pallas_call x1 -> x2, Pallas kernels: 83.9 us -> 80.1 us  [the longest x1 78.8 us: per_device(): pl.pallas_call(functools.partial(kernel, ni, nj, nk, counts), out_shape=j...]
    unnamed x7 -> x0, local copies, waits for them, and re-layouts: 3.13 us -> none
where the time goes in v4:
time: 80.9 us; the launch traced here: 80.7 us
  Pallas kernels  80.1 us (99%)
    pallas_call x1, Pallas kernels, per_device(): pl.pallas_call(functools.partial(kernel, ni, nj, nk, counts), out_shape=j...  78.8 us

profile of v4, /device:TPU:1, one launch (start us, length us, event | category | flops | bytes accessed | tf_op | source)
XLA Modules:
  0.0 80.7 jit_solution(16152554698965406971)
XLA Ops:
  0.6 78.8 %shard_map.58.in_ref = f32[10,256]{1,0:T(8,128)} custom-call(f32[16384,128]{1,0:T(8,128)} %bitcast.1, f32[4,256]{1,0:T(4,128)} %b_hbm.1, f32[2,256]{1,0:T(2,128)} %c_hbm.1), custom_call_target="tpu_custom_call" | custom-call | tf_op jit(solution)/shard_map/pallas_call | solution.py:468
  79.4 1.3 %shard_map.59 = (f32[4,256]{1,0:T(4,128)}, f32[4,256]{1,0:T(4,128)}, f32[2,256]{1,0:T(2,128)}) custom-call(f32[10,256]{1,0:T(8,128)} %shard_map.58.in_ref), custom_call_target="tpu_custom_call" | custom-call | tf_op jit(solution)/shard_map/pallas_call | solution.py:478

commit v5 on v4

--- a/solution.py
+++ b/solution.py
@@ -14,7 +14,7 @@
 PIV = 64
 BLOCK = 16
 GROUP = 32
-SERVE = 2
+SERVE = 1
 SERVE_B = 2
 SERVE_C = 1
 TURNS = 80
@@ -147,14 +147,13 @@
 
 def unit_diagonal(matrix):
     along, down = diagonals(matrix)
-    along, down = 1.0 / jnp.sqrt(along), 1.0 / jnp.sqrt(down)
-    return (matrix * along) * down, along
+    return (matrix * (1.0 / jnp.sqrt(along))) * (1.0 / jnp.sqrt(down)), along
 
 
 def kernel(
     ni, nj, nk, counts,
     x_hbm, b_hbm, c_hbm, out_ref,
-    xs, xt, ys, bin_, cin, bblk, cblk, ablk, nblk, whi, wlo, rows, fac, arow, hrow,
+    xs, xt, ys, bin_, cin, bblk, cblk, ablk, nblk, whi, wlo, rows, fac, sol_b, arow, hrow, crow, scales,
     part_a, part_b, part_c, recv_a, recv_b, recv_c, own_a, own_b, own_c, gat_a, gat_b, gat_c,
     bx, cy, nx, half_b, half_c, half_n, other_b, other_c, other_n,
     gp_a, ex_a, sum_a, g_a, gcm, hmat, gca, nrm, own_n,
@@ -196,14 +195,21 @@
     def send(phase, n, me, peer, src_of, dst, buf):
         started.append((phase, n, me, peer, buf))
 
-        def go(p, carry):
+        def copy_to(p):
             q = lax.rem(me + p, n)
             pltpu.make_async_remote_copy(
                 src_ref=src_of(q), dst_ref=dst, send_sem=ss.at[phase], recv_sem=rs.at[phase],
                 device_id=peer(q), device_id_type=MESH,
             ).start()
+
+        def both_ways(t, carry):
+            copy_to(n // 2 - t)
+            copy_to(n // 2 + t)
             return carry
-        lax.fori_loop(1, n, go, 0)
+
+        copy_to(n // 2)
+        if n > 2:
+            lax.fori_loop(1, n // 2, both_ways, 0)
 
     def all_of(phase, n, me, peer, buf):
         some = buf.at[pl.ds(0, n - 1)]
@@ -324,8 +330,12 @@
     all_of(4, nx_, x, line_x, bx).wait_recv()
     half_b[...] = gram_of(bx[...].reshape(nx_ * 128, rank))
     swap(8, half_b, other_b)
-    gcm[...] = swapped(7, half_c, other_c)
-    hmat[...], hrow[...] = unit_diagonal(swapped(8, half_b, other_b) * gcm[...])
+    unit_c, diag_c = unit_diagonal(swapped(7, half_c, other_c))
+    gcm[...] = unit_c
+    crow[...] = 1.0 / jnp.sqrt(diag_c)
+    unit_b, diag_b = unit_diagonal(swapped(8, half_b, other_b))
+    hmat[...] = unit_b * gcm[...]
+    hrow[...] = (1.0 / jnp.sqrt(diag_b)) * crow[...]
     invert_in(hmat, 0, SERVE)
     all_of(6, n_a, me_a, peer_a, recv_a).wait_recv()
     own_a[...] = jnp.sum(recv_a[...], axis=0)
@@ -375,14 +385,15 @@
 
     all_of(11, n_a, me_a, peer_a, g_a).wait_recv()
     gram = g_a[...].reshape(rank, rank)
-    along, down = diagonals(gram)
-    scale_a = jnp.sqrt(along / counts[0] + 1e-06)
-    inverse_a = 1.0 / scale_a
-    gca[...] = (gram * inverse_a) * (1.0 / jnp.sqrt(down / counts[0] + 1e-06))
-    hmat[...], hrow[...] = unit_diagonal(gca[...] * gcm[...])
-    r_a, r_b, r_c = own_a.shape[0], own_b.shape[0], own_c.shape[0]
-    out_ref[0:r_a, :] = own_rows(ablk, me_a, r_a) / scale_a
-    arow[...] = inverse_a
+    unit_a, diag_a = unit_diagonal(gram)
+    gca[...] = unit_a
+    hmat[...] = unit_a * gcm[...]
+    scale_a = jnp.sqrt(diag_a / counts[0] + 1e-06)
+    ratio_a = scale_a / jnp.sqrt(diag_a)
+    hrow[...] = ratio_a * crow[...]
+    crow[...] = ratio_a
+    arow[...] = 1.0 / scale_a
+    scales[0:1, :] = scale_a
     invert_in(hmat, 0, SERVE_B)
     all_of(13, n_b, me_b, peer_b, gat_b).wait_recv()
     assemble(nblk, gat_b)
@@ -390,7 +401,7 @@
     send(14, nx_, x, line_x, lambda q: nblk, nx.at[x], nx)
     invert_in(hmat, SERVE_B)
     raw_b = solve(nblk[...] * arow[...])
-    ablk[...] = raw_b
+    sol_b[...] = raw_b
 
     fac[...] = raw_b * arow[...]
     rows[...] = sum_rows(fac)
@@ -402,12 +413,12 @@
     half_n[...] = gram_of(solve(nx[...].reshape(nx_ * 128, rank) * arow[...]))
     swap(16, half_n, other_n)
     gram = swapped(16, half_n, other_n)
-    along, down = diagonals(gram)
-    scale_b = jnp.sqrt(along / counts[1] + 1e-06)
-    inverse_b = 1.0 / scale_b
-    hmat[...], hrow[...] = unit_diagonal(gca[...] * ((gram * inverse_b) * (1.0 / jnp.sqrt(down / counts[1] + 1e-06))))
-    out_ref[r_a : r_a + r_b, :] = own_rows(ablk, me_b, r_b) / scale_b
-    arow[...] = inverse_b
+    unit_n, diag_n = unit_diagonal(gram)
+    hmat[...] = gca[...] * unit_n
+    scale_b = jnp.sqrt(diag_n / counts[1] + 1e-06)
+    hrow[...] = crow[...] * (scale_b / jnp.sqrt(diag_n))
+    arow[...] = 1.0 / scale_b
+    scales[1:2, :] = scale_b
     invert_in(hmat, 0, SERVE_C)
     all_of(15, n_c, me_c, peer_c, recv_c).wait_recv()
     own_c[...] = jnp.sum(recv_c[...], axis=0)
@@ -423,6 +434,9 @@
     own_n[...] = squares
     nrm[me_a] = squares
     send(18, n_a, me_a, peer_a, lambda q: own_n, nrm.at[me_a], nrm)
+    r_a, r_b, r_c = own_a.shape[0], own_b.shape[0], own_c.shape[0]
+    out_ref[0:r_a, :] = own_rows(ablk, me_a, r_a) / scales[0:1, :]
+    out_ref[r_a : r_a + r_b, :] = own_rows(sol_b, me_b, r_b) / scales[1:2, :]
     mine_c = raw_c[0:per]
     for t in range(1, ni):
         mine_c = jnp.where(ia == t, raw_c[t * per : (t + 1) * per], mine_c)
@@ -453,7 +467,7 @@
         v(nk, ni, r_b, rank), v(nj, ni, r_c, rank),
         v(128, rank), v(128, rank), v(128, rank), v(128, rank),
         pltpu.VMEM((256, rank), BF16), pltpu.VMEM((256, rank), BF16),
-        v(128, rank), v(128, rank), v(1, rank), v(1, rank),
+        v(128, rank), v(128, rank), v(128, rank), v(1, rank), v(1, rank), v(1, rank), v(8, rank),
         v(n_a, r_a, rank), v(n_b, r_b, rank), v(n_c, r_c, rank),
         v(n_a, r_a, rank), v(n_b, r_b, rank), v(n_c, r_c, rank),
         v(r_a, rank), v(r_b, rank), v(r_c, rank),

time: 80.9 us -> 77.9 us (0.963)
  Pallas kernels: 80.1 us -> 77 us
    pallas_call x1, Pallas kernels: 78.8 us -> 75.7 us  [per_device(): pl.pallas_call(functools.partial(kernel, ni, nj, nk, counts), out_shape=j...]
where the time goes in v5:
time: 77.9 us; the launch traced here: 77.7 us
  Pallas kernels  77 us (99%)
    pallas_call x1, Pallas kernels, per_device(): pl.pallas_call(functools.partial(kernel, ni, nj, nk, counts), out_shape=j...  75.7 us

profile of v5, /device:TPU:1, one launch (start us, length us, event | category | flops | bytes accessed | tf_op | source)
XLA Modules:
  0.0 77.7 jit_solution(9497409229713288815)
XLA Ops:
  0.6 75.7 %shard_map.58.in_ref = f32[10,256]{1,0:T(8,128)} custom-call(f32[16384,128]{1,0:T(8,128)} %bitcast.1, f32[4,256]{1,0:T(4,128)} %b_hbm.1, f32[2,256]{1,0:T(2,128)} %c_hbm.1), custom_call_target="tpu_custom_call" | custom-call | tf_op jit(solution)/shard_map/pallas_call | solution.py:482
  76.3 1.3 %shard_map.59 = (f32[4,256]{1,0:T(4,128)}, f32[4,256]{1,0:T(4,128)}, f32[2,256]{1,0:T(2,128)}) custom-call(f32[10,256]{1,0:T(8,128)} %shard_map.58.in_ref), custom_call_target="tpu_custom_call" | custom-call | tf_op jit(solution)/shard_map/pallas_call | solution.py:492

commit v6 on v5

--- a/solution.py
+++ b/solution.py
@@ -209,7 +209,7 @@
 
         copy_to(n // 2)
         if n > 2:
-            lax.fori_loop(1, n // 2, both_ways, 0)
+            lax.fori_loop(1, n // 2, both_ways, 0, unroll=True)
 
     def all_of(phase, n, me, peer, buf):
         some = buf.at[pl.ds(0, n - 1)]
@@ -252,10 +252,13 @@
     barrier = pltpu.get_barrier_semaphore()
 
     def hello(n, me, peer):
-        def go(p, carry):
+        def signal_to(p):
             pl.semaphore_signal(barrier, inc=1, device_id=peer(lax.rem(me + p, n)), device_id_type=MESH)
-            return carry
-        lax.fori_loop(1, n, go, 0)
+
+        signal_to(n // 2)
+        for t in range(1, n // 2):
+            signal_to(n // 2 - t)
+            signal_to(n // 2 + t)
 
     hello(ni, ia, line_i)
     hello(nj, ja, line_j)

time: 77.9 us -> 77.5 us (level)
  no operation moved by 1% of the time
where the time goes in v6:
time: 77.5 us; the launch traced here: 77.3 us
  Pallas kernels  76.6 us (99%)
    pallas_call x1, Pallas kernels, per_device(): pl.pallas_call(functools.partial(kernel, ni, nj, nk, counts), out_shape=j...  75.3 us

profile of v6, /device:TPU:1, one launch (start us, length us, event | category | flops | bytes accessed | tf_op | source)
XLA Modules:
  0.0 77.3 jit_solution(424010222692037585)
XLA Ops:
  0.6 75.3 %shard_map.58.in_ref = f32[10,256]{1,0:T(8,128)} custom-call(f32[16384,128]{1,0:T(8,128)} %bitcast.1, f32[4,256]{1,0:T(4,128)} %b_hbm.1, f32[2,256]{1,0:T(2,128)} %c_hbm.1), custom_call_target="tpu_custom_call" | custom-call | tf_op jit(solution)/shard_map/pallas_call | solution.py:485
  76.0 1.3 %shard_map.59 = (f32[4,256]{1,0:T(4,128)}, f32[4,256]{1,0:T(4,128)}, f32[2,256]{1,0:T(2,128)}) custom-call(f32[10,256]{1,0:T(8,128)} %shard_map.58.in_ref), custom_call_target="tpu_custom_call" | custom-call | tf_op jit(solution)/shard_map/pallas_call | solution.py:495
